TPU v7x, 128 devices: a whole 4x4x4 slice. The times are simulated.
128 devices in a mesh: dp: 16 (over z_hi, y, core), tensor: 8 (over z_lo, x).
Axes of the slice: x: 4, y: 4, z: 4 (z_hi: 2, z_lo: 2; z = z_hi * 2 + z_lo), core: 2. Of those that a mesh axis runs over, the one named last changes fastest.
Arguments:
- layer_in: bfloat16 [16384, 2048], P(('dp', 'tensor')), may hold values from -6 to 6
- cotangent: bfloat16 [16384, 2048], P(('dp', 'tensor')), may hold values from -6 to 6
- seq_lengths: int32 [16, 4], P('dp'), may hold values from 1 to 768, 1024 in all within a row
- w_qkv: float32 [2048, 3, 2048], P('dp', None, 'tensor'), may hold values from -0.125 to 0.125
- w_out: float32 [2048, 2048], P('tensor', 'dp'), may hold values from -0.75 to 0.75
- w_up: float32 [2048, 8192], P('dp', 'tensor'), may hold values from -0.125 to 0.125
- w_down: float32 [8192, 2048], P('tensor', 'dp'), may hold values from -0.0625 to 0.0625
- b_qkv: float32 [3, 2048], P(None, 'tensor'), may hold values from -1.75 to 1.75
- b_up: float32 [8192], P('tensor'), may hold values from -1.75 to 1.75
- norm_gains: float32 [2, 2048], replicated, may hold values from 0.5 to 1.5
- row_biases: float32 [4, 2048], replicated, may hold values from -1.25 to 1.25
- m_qkv: float32 [2048, 3, 2048], P('dp', None, 'tensor'), may hold values from -80 to 80
- v_qkv: float32 [2048, 3, 2048], P('dp', None, 'tensor'), may hold values from 868.352 to 3440.64
- m_out: float32 [2048, 2048], P('tensor', 'dp'), may hold values from -24 to 24
- v_out: float32 [2048, 2048], P('tensor', 'dp'), may hold values from 78.6432 to 311.296
- m_up: float32 [2048, 8192], P('dp', 'tensor'), may hold values from -32 to 32
- v_up: float32 [2048, 8192], P('dp', 'tensor'), may hold values from 106.496 to 425.984
- m_down: float32 [8192, 2048], P('tensor', 'dp'), may hold values from -56 to 56
- v_down: float32 [8192, 2048], P('tensor', 'dp'), may hold values from 360.448 to 1458.176
- m_bqkv: float32 [3, 2048], P(None, 'tensor'), may hold values from -80 to 80
- v_bqkv: float32 [3, 2048], P(None, 'tensor'), may hold values from 868.352 to 3440.64
- m_bup: float32 [8192], P('tensor'), may hold values from -32 to 32
- v_bup: float32 [8192], P('tensor'), may hold values from 106.496 to 425.984
- m_gains: float32 [2, 2048], replicated, may hold values from -96 to 96
- v_gains: float32 [2, 2048], replicated, may hold values from 1245.184 to 4915.2
- m_biases: float32 [4, 2048], replicated, may hold values from -80 to 80
- v_biases: float32 [4, 2048], replicated, may hold values from 868.352 to 3440.64
Outputs:
- out_rows: bfloat16 [16384, 2048], P(('dp', 'tensor'))
- input_grad: float32 [16384, 2048], P(('dp', 'tensor'))
- qkv_first: float32 [2048, 3, 2048], P('dp', None, 'tensor')
- qkv_second: float32 [2048, 3, 2048], P('dp', None, 'tensor')
- qkv_new: float32 [2048, 3, 2048], P('dp', None, 'tensor')
- out_first: float32 [2048, 2048], P('tensor', 'dp')
- out_second: float32 [2048, 2048], P('tensor', 'dp')
- out_new: float32 [2048, 2048], P('tensor', 'dp')
- up_first: float32 [2048, 8192], P('dp', 'tensor')
- up_second: float32 [2048, 8192], P('dp', 'tensor')
- up_new: float32 [2048, 8192], P('dp', 'tensor')
- down_first: float32 [8192, 2048], P('tensor', 'dp')
- down_second: float32 [8192, 2048], P('tensor', 'dp')
- down_new: float32 [8192, 2048], P('tensor', 'dp')
- bqkv_first: float32 [3, 2048], P(None, 'tensor')
- bqkv_second: float32 [3, 2048], P(None, 'tensor')
- bqkv_new: float32 [3, 2048], P(None, 'tensor')
- bup_first: float32 [8192], P('tensor')
- bup_second: float32 [8192], P('tensor')
- bup_new: float32 [8192], P('tensor')
- gains_first: float32 [2, 2048], replicated
- gains_second: float32 [2, 2048], replicated
- gains_new: float32 [2, 2048], replicated
- biases_first: float32 [4, 2048], replicated
- biases_second: float32 [4, 2048], replicated
- biases_new: float32 [4, 2048], replicated
Inputs may be any that keep to these rules, and one draw needn't show every extreme that they name: `seq_lengths`: each row lists the lengths of the 4 sequences packed in one data group in order; a row sums to 1024 and its longest length is exactly 768.
All inputs are finite; a program needn't handle non-finite values.
Results may differ from a plain program's by a relative error of at most 0.025.
Values may be sent and summed in bfloat16 or wider, within the bound.
A program may use at most 128 MiB of HBM per device.

v0:
```python
import math

import jax
import jax.numpy as jnp
from jax import lax
from jax.sharding import PartitionSpec as P

HEAD_DIM = 256
ROT = 64
STEP = 10


NORM_EPS = 1e-05
BETA_ONE = 0.9
BETA_TWO = 0.95
ADAM_EPS = 1e-08
STEP_RATES = (0.04, 0.2, 0.04, 0.02, 0.3, 0.3, 0.5, 0.3)
DECAY_RATES = (0.01, 0.01, 0.01, 0.01, 0.0, 0.0, 0.0, 0.0)


def segment_info(lengths, token_count):
    indices = jnp.arange(token_count, dtype=jnp.int32)
    ends = jnp.cumsum(lengths)
    starts = ends - lengths
    segment = jnp.sum((indices[:, None] >= ends[None, :]).astype(jnp.int32), axis=1)
    own_seq = (segment[:, None] == jnp.arange(lengths.shape[0], dtype=jnp.int32)[None, :]).astype(
        jnp.int32
    )
    position = indices - jnp.sum(own_seq * starts[None, :], axis=1)
    return (segment, position)


def rotary_tables(position, rot_dims):
    half_rot = rot_dims // 2
    frequency = 10000.0 ** (-jnp.arange(half_rot, dtype=jnp.float32) * 2.0 / rot_dims)
    angles = position.astype(jnp.float32)[:, None] * frequency[None, :]
    angles = jnp.concatenate([angles, angles], axis=1)
    return (jnp.cos(angles), jnp.sin(angles))


def rotate(tensor_in, cosines, sine_rows, rot_dims):
    half_rot = rot_dims // 2
    rotated = tensor_in[..., :rot_dims]
    turned = jnp.concatenate([-rotated[..., half_rot:], rotated[..., :half_rot]], axis=-1)
    moved = rotated * cosines[:, None, :] + turned * sine_rows[:, None, :]
    return jnp.concatenate([moved, tensor_in[..., rot_dims:]], axis=-1)


def turn_back(grad_in, cosines, sine_rows, rot_dims):
    half_rot = rot_dims // 2
    rotated = grad_in[..., :rot_dims]
    sined = rotated * sine_rows[:, None, :]
    turned = jnp.concatenate([sined[..., half_rot:], -sined[..., :half_rot]], axis=-1)
    moved = rotated * cosines[:, None, :] + turned
    return jnp.concatenate([moved, grad_in[..., rot_dims:]], axis=-1)


def gelu_slope(inner_pre):
    normal_cdf = 0.5 * (1.0 + lax.erf(inner_pre * (1.0 / math.sqrt(2.0))))
    density = jnp.exp(-0.5 * inner_pre * inner_pre) * (1.0 / math.sqrt(2.0 * math.pi))
    return normal_cdf + inner_pre * density


def over_rows(left, right):
    return lax.dot_general(
        left, right, (((0,), (0,)), ((), ())), preferred_element_type=jnp.float32
    )


def by_rows(left, right):
    return lax.dot_general(
        left, right, (((1,), (1,)), ((), ())), preferred_element_type=jnp.float32
    )


def allowed_mask(query_segment, query_index, segment, indices):
    return (query_segment[:, None] == segment[None, :]) & (query_index[:, None] >= indices[None, :])


def attend_forward(queries, keys_low, values, segment, block_rows, score_scale):
    token_count, head_count, head_size = queries.shape
    block_count = token_count // block_rows
    indices = jnp.arange(token_count, dtype=jnp.int32)

    def one_block(block_args):
        query_block, query_segment, query_index = block_args
        scores = (
            jnp.einsum("qhd,khd->hqk", query_block, keys_low, preferred_element_type=jnp.float32)
            * score_scale
        )
        allowed = allowed_mask(query_segment, query_index, segment, indices)
        scores = jnp.where(allowed[None], scores, -jnp.inf)
        row_max = jnp.max(scores, axis=-1, keepdims=True)
        expo = jnp.exp(scores - row_max)
        row_total = jnp.sum(expo, axis=-1, keepdims=True)
        probs = (expo / row_total).astype(jnp.bfloat16)
        result = jnp.einsum("hqk,khd->qhd", probs, values, preferred_element_type=jnp.float32)
        return (result, (row_max + jnp.log(row_total))[..., 0])

    mixed, log_total = lax.map(
        one_block,
        (
            queries.reshape(block_count, block_rows, head_count, head_size),
            segment.reshape(block_count, block_rows),
            indices.reshape(block_count, block_rows),
        ),
    )
    return (mixed.reshape(token_count, head_count, head_size), log_total)


def attend_backward(
    queries, keys_low, values, mixed_grad, log_total, segment, block_rows, score_scale
):
    token_count, head_count, head_size = queries.shape
    block_count = token_count // block_rows
    indices = jnp.arange(token_count, dtype=jnp.int32)

    def one_block(running, block_args):
        key_grad, value_grad = running
        query_block, grad_block, block_total, query_segment, query_index = block_args
        scores = (
            jnp.einsum("qhd,khd->hqk", query_block, keys_low, preferred_element_type=jnp.float32)
            * score_scale
        )
        allowed = allowed_mask(query_segment, query_index, segment, indices)
        scores = jnp.where(allowed[None], scores, -jnp.inf)
        probs = jnp.exp(scores - block_total[..., None])
        prob_grad = jnp.einsum(
            "qhd,khd->hqk", grad_block, values, preferred_element_type=jnp.float32
        )
        row_delta = jnp.sum(probs * prob_grad, axis=-1, keepdims=True)
        score_grad = (probs * (prob_grad - row_delta)).astype(jnp.bfloat16)
        query_grad = (
            jnp.einsum("hqk,khd->qhd", score_grad, keys_low, preferred_element_type=jnp.float32)
            * score_scale
        )
        key_grad = (
            key_grad
            + jnp.einsum(
                "hqk,qhd->khd", score_grad, query_block, preferred_element_type=jnp.float32
            )
            * score_scale
        )
        value_grad = value_grad + jnp.einsum(
            "hqk,qhd->khd",
            probs.astype(jnp.bfloat16),
            grad_block,
            preferred_element_type=jnp.float32,
        )
        return ((key_grad, value_grad), query_grad)

    zero_rows = jnp.zeros((token_count, head_count, head_size), jnp.float32)
    block_shape = (block_count, block_rows, head_count, head_size)
    (key_grad, value_grad), query_grad = lax.scan(
        one_block,
        (zero_rows, zero_rows),
        (
            queries.reshape(block_shape),
            mixed_grad.reshape(block_shape),
            log_total,
            segment.reshape(block_count, block_rows),
            indices.reshape(block_count, block_rows),
        ),
    )
    return (query_grad.reshape(token_count, head_count, head_size), key_grad, value_grad)


def adam_step(weight, gradient, moment_one, moment_two, step_rate, decay_rate):
    moment_one = BETA_ONE * moment_one + (1.0 - BETA_ONE) * gradient
    moment_two = BETA_TWO * moment_two + (1.0 - BETA_TWO) * gradient * gradient
    ratio = (
        moment_one
        / (1.0 - BETA_ONE**STEP)
        / (jnp.sqrt(moment_two / (1.0 - BETA_TWO**STEP)) + ADAM_EPS)
    )
    return (moment_one, moment_two, weight - step_rate * (ratio + decay_rate * weight))


def local(
    layer_in,
    cotangent,
    seq_lengths,
    w_qkv,
    w_out,
    w_up,
    w_down,
    b_qkv,
    b_up,
    norm_gains,
    row_biases,
    m_qkv,
    v_qkv,
    m_out,
    v_out,
    m_up,
    v_up,
    m_down,
    v_down,
    m_bqkv,
    v_bqkv,
    m_bup,
    v_bup,
    m_gains,
    v_gains,
    m_biases,
    v_biases,
):
    tensor_size = lax.axis_size("tensor")
    tensor_place = lax.axis_index("tensor")
    row_count = layer_in.shape[0]
    group_rows = row_count * tensor_size
    model_width = layer_in.shape[1]
    head_cols = w_qkv.shape[2]
    unit_cols = w_up.shape[1]
    head_count = head_cols // HEAD_DIM
    score_scale = HEAD_DIM ** (-0.5)
    block_rows = min(512, group_rows)
    resid = layer_in.astype(jnp.float32)
    row_mean = jnp.mean(resid, axis=-1, keepdims=True)
    centered = resid - row_mean
    variance = jnp.mean(centered * centered, axis=-1, keepdims=True)
    inverse = lax.rsqrt(variance + NORM_EPS)
    unit = centered * inverse
    unit_low = unit.astype(jnp.bfloat16)
    sent = (
        w_qkv.astype(jnp.bfloat16),
        w_out.astype(jnp.bfloat16),
        w_up.astype(jnp.bfloat16),
        w_down.astype(jnp.bfloat16),
    )
    qkv_full, out_full, up_full, down_full = (
        lax.all_gather(sent[0], "dp", axis=0, tiled=True),
        lax.all_gather(sent[1], "dp", axis=1, tiled=True),
        lax.all_gather(sent[2], "dp", axis=0, tiled=True),
        lax.all_gather(sent[3], "dp", axis=1, tiled=True),
    )
    unit_own = unit_low.astype(jnp.float32)
    first_local = (unit_own * norm_gains[0] + row_biases[0]).astype(jnp.bfloat16)
    second_local = (unit_own * norm_gains[1] + row_biases[1]).astype(jnp.bfloat16)
    first_normed, second_normed = (
        lax.all_gather(first_local, "tensor", axis=0, tiled=True),
        lax.all_gather(second_local, "tensor", axis=0, tiled=True),
    )
    segment, position = segment_info(seq_lengths[0], group_rows)
    cosines, sine_rows = rotary_tables(position, ROT)
    qkv_flat = qkv_full.reshape(model_width, 3 * head_cols)
    projected = jnp.dot(first_normed, qkv_flat, preferred_element_type=jnp.float32).reshape(
        group_rows, 3, head_count, HEAD_DIM
    )
    projected = projected + b_qkv.reshape(1, 3, head_count, HEAD_DIM)
    queries = rotate(projected[:, 0], cosines, sine_rows, ROT).astype(jnp.bfloat16)
    keys_low = rotate(projected[:, 1], cosines, sine_rows, ROT).astype(jnp.bfloat16)
    values = projected[:, 2].astype(jnp.bfloat16)
    mixed, log_total = attend_forward(queries, keys_low, values, segment, block_rows, score_scale)
    mixed_low = mixed.reshape(group_rows, head_cols).astype(jnp.bfloat16)
    inner_pre = jnp.dot(second_normed, up_full, preferred_element_type=jnp.float32) + b_up
    activation = jax.nn.gelu(inner_pre, approximate=False).astype(jnp.bfloat16)
    branch = lax.psum_scatter(
        (
            jnp.dot(mixed_low, out_full, preferred_element_type=jnp.float32)
            + jnp.dot(activation, down_full, preferred_element_type=jnp.float32)
        ).astype(jnp.bfloat16),
        "tensor",
        scatter_dimension=0,
        tiled=True,
    ).astype(jnp.float32)
    out_rows = (resid + branch + row_biases[2] + row_biases[3]).astype(jnp.bfloat16)
    qkv_full, out_full, up_full, down_full = (
        lax.all_gather(sent[0], "dp", axis=0, tiled=True),
        lax.all_gather(sent[1], "dp", axis=1, tiled=True),
        lax.all_gather(sent[2], "dp", axis=0, tiled=True),
        lax.all_gather(sent[3], "dp", axis=1, tiled=True),
    )
    qkv_flat = qkv_full.reshape(model_width, 3 * head_cols)
    grad_rows = lax.all_gather(cotangent, "tensor", axis=0, tiled=True)
    out_grad = over_rows(mixed_low, grad_rows)
    down_grad = over_rows(activation, grad_rows)
    mixed_grad = (
        by_rows(grad_rows, out_full).astype(jnp.bfloat16).reshape(group_rows, head_count, HEAD_DIM)
    )
    inner_grad = by_rows(grad_rows, down_full) * gelu_slope(inner_pre)
    inner_low = inner_grad.astype(jnp.bfloat16)
    up_grad = over_rows(second_normed, inner_low)
    second_part = by_rows(inner_low, up_full)
    query_grad, key_grad, value_grad = attend_backward(
        queries, keys_low, values, mixed_grad, log_total, segment, block_rows, score_scale
    )
    projected_grad = jnp.stack(
        [
            turn_back(query_grad, cosines, sine_rows, ROT),
            turn_back(key_grad, cosines, sine_rows, ROT),
            value_grad,
        ],
        axis=1,
    )
    projected_grad = projected_grad.reshape(group_rows, 3 * head_cols)
    projected_low = projected_grad.astype(jnp.bfloat16)
    qkv_grad = over_rows(first_normed, projected_low).reshape(model_width, 3, head_cols)
    first_part = by_rows(projected_low, qkv_flat)
    qkv_bias_grad = jnp.sum(projected_grad, axis=0).reshape(3, head_cols)
    up_bias_grad = jnp.sum(inner_grad, axis=0)
    grad_own = cotangent.astype(jnp.float32)
    out_bias_grad = jnp.sum(grad_own, axis=0)
    first_grad, second_grad = (
        lax.psum_scatter(
            first_part.astype(jnp.bfloat16), "tensor", scatter_dimension=0, tiled=True
        ).astype(jnp.float32),
        lax.psum_scatter(
            second_part.astype(jnp.bfloat16), "tensor", scatter_dimension=0, tiled=True
        ).astype(jnp.float32),
    )
    unit_own = unit_low.astype(jnp.float32)
    gain_part = jnp.stack(
        [jnp.sum(first_grad * unit_own, axis=0), jnp.sum(second_grad * unit_own, axis=0)]
    )
    shift_part = jnp.stack([jnp.sum(first_grad, axis=0), jnp.sum(second_grad, axis=0)])
    unit_grad = first_grad * norm_gains[0] + second_grad * norm_gains[1]
    unit_mean = jnp.mean(unit_grad, axis=-1, keepdims=True)
    unit_proj = jnp.mean(unit_grad * unit, axis=-1, keepdims=True)
    input_grad = grad_own + inverse * (unit_grad - unit_mean - unit * unit_proj)
    bias_part = jnp.concatenate(
        [shift_part, out_bias_grad[None, :], out_bias_grad[None, :]], axis=0
    )
    own_slot = (jnp.arange(tensor_size, dtype=jnp.int32) == tensor_place).astype(jnp.float32)
    qkv_bias_all = (own_slot[None, :, None] * qkv_bias_grad[:, None, :]).reshape(
        3, tensor_size * head_cols
    )
    up_bias_all = (own_slot[:, None] * up_bias_grad[None, :]).reshape(tensor_size * unit_cols)
    gain_sum, bias_sum, qkv_bias_sum, up_bias_sum = lax.psum(
        (gain_part, bias_part, qkv_bias_all, up_bias_all), ("dp", "tensor")
    )
    qkv_bias_sum = lax.dynamic_slice_in_dim(qkv_bias_sum, tensor_place * head_cols, head_cols, 1)
    up_bias_sum = lax.dynamic_slice_in_dim(up_bias_sum, tensor_place * unit_cols, unit_cols, 0)
    qkv_sum, out_sum, up_sum, down_sum = (
        lax.psum_scatter(
            qkv_grad.astype(jnp.bfloat16), "dp", scatter_dimension=0, tiled=True
        ).astype(jnp.float32),
        lax.psum_scatter(
            out_grad.astype(jnp.bfloat16), "dp", scatter_dimension=1, tiled=True
        ).astype(jnp.float32),
        lax.psum_scatter(
            up_grad.astype(jnp.bfloat16), "dp", scatter_dimension=0, tiled=True
        ).astype(jnp.float32),
        lax.psum_scatter(
            down_grad.astype(jnp.bfloat16), "dp", scatter_dimension=1, tiled=True
        ).astype(jnp.float32),
    )
    params = (w_qkv, w_out, w_up, w_down, b_qkv, b_up, norm_gains, row_biases)
    grad_list = (qkv_sum, out_sum, up_sum, down_sum, qkv_bias_sum, up_bias_sum, gain_sum, bias_sum)
    moments = (
        (m_qkv, v_qkv),
        (m_out, v_out),
        (m_up, v_up),
        (m_down, v_down),
        (m_bqkv, v_bqkv),
        (m_bup, v_bup),
        (m_gains, v_gains),
        (m_biases, v_biases),
    )
    updated = []
    for which in range(8):
        updated.append(
            adam_step(
                params[which],
                grad_list[which],
                moments[which][0],
                moments[which][1],
                STEP_RATES[which],
                DECAY_RATES[which],
            )
        )
    return (
        out_rows,
        input_grad,
        updated[0][0],
        updated[0][1],
        updated[0][2],
        updated[1][0],
        updated[1][1],
        updated[1][2],
        updated[2][0],
        updated[2][1],
        updated[2][2],
        updated[3][0],
        updated[3][1],
        updated[3][2],
        updated[4][0],
        updated[4][1],
        updated[4][2],
        updated[5][0],
        updated[5][1],
        updated[5][2],
        updated[6][0],
        updated[6][1],
        updated[6][2],
        updated[7][0],
        updated[7][1],
        updated[7][2],
    )


def solution(mesh):
    return jax.shard_map(
        local,
        mesh=mesh,
        in_specs=(
            P(("dp", "tensor"), None),
            P(("dp", "tensor"), None),
            P("dp", None),
            P("dp", None, "tensor"),
            P("tensor", "dp"),
            P("dp", "tensor"),
            P("tensor", "dp"),
            P(None, "tensor"),
            P("tensor"),
            P(),
            P(),
            P("dp", None, "tensor"),
            P("dp", None, "tensor"),
            P("tensor", "dp"),
            P("tensor", "dp"),
            P("dp", "tensor"),
            P("dp", "tensor"),
            P("tensor", "dp"),
            P("tensor", "dp"),
            P(None, "tensor"),
            P(None, "tensor"),
            P("tensor"),
            P("tensor"),
            P(),
            P(),
            P(),
            P(),
        ),
        out_specs=(
            P(("dp", "tensor"), None),
            P(("dp", "tensor"), None),
            P("dp", None, "tensor"),
            P("dp", None, "tensor"),
            P("dp", None, "tensor"),
            P("tensor", "dp"),
            P("tensor", "dp"),
            P("tensor", "dp"),
            P("dp", "tensor"),
            P("dp", "tensor"),
            P("dp", "tensor"),
            P("tensor", "dp"),
            P("tensor", "dp"),
            P("tensor", "dp"),
            P(None, "tensor"),
            P(None, "tensor"),
            P(None, "tensor"),
            P("tensor"),
            P("tensor"),
            P("tensor"),
            P(),
            P(),
            P(),
            P(),
            P(),
            P(),
        ),
        check_vma=False,
    )
```

profile of v0, /device:TPU:0, one launch (start us, length us, event | category | flops | bytes accessed | tf_op | source)
XLA Modules:
  0.0 1026.9 jit_solution(9542055002500865480)
XLA Ops:
  7.3 1.9 copy.85
  14.2 2.5 fusion.75
  19.5 48.2 %all-gather.10.cloned.1.call-done = bf16[2048,3,256]{0,2,1:T(8,128)(2,1)} async-done(((bf16[128,3,256]{0,2,1:T(8,128)(2,1)}), bf16[2048,3,256]{0,2,1:T(8,128)(2,1)}) %all-gather.10.cloned.1.call-update) | async-done | bytes 3145744 | tf_op jit(solution)/shard_map/all_gather | solution.py:232
  67.7 53.4 %all-gather.8.cloned.1.call-done = bf16[1024,2048]{1,0:T(8,128)(2,1)} async-done(((bf16[128,2048]{1,0:T(8,128)(2,1)}), bf16[1024,2048]{1,0:T(8,128)(2,1)}) %all-gather.8.cloned.1.call-update) | async-done | bytes 4194320 | tf_op jit(solution)/shard_map/all_gather | solution.py:241
  121.1 8.3 add_bitcast_fusion.1
  136.9 8.2 while.30
  136.9 1.9 fusion.189
  139.3 1.6 fusion.191
  141.0 1.9 fusion.189
  143.4 1.6 fusion.191
  145.1 29.1 %all-gather.20.cloned.1.call-done = bf16[1024,2048]{1,0:T(8,128)(2,1)} async-done(((bf16[128,2048]{1,0:T(8,128)(2,1)}), bf16[1024,2048]{1,0:T(8,128)(2,1)}) %all-gather.20.cloned.1.call-update) | async-done | bytes 4194320 | tf_op jit(solution)/shard_map/all_gather | solution.py:275
  174.1 3.5 convolution_convert_fusion.4
  179.3 48.3 %all-gather.14.cloned.1.call-done = bf16[1024,2048]{1,0:T(8,128)(2,1)} async-done(((bf16[128,2048]{1,0:T(8,128)(2,1)}), bf16[1024,2048]{1,0:T(8,128)(2,1)}) %all-gather.14.cloned.1.call-update) | async-done | bytes 4194320 | tf_op jit(solution)/shard_map/all_gather | solution.py:242
  227.6 57.7 %all-gather.16.cloned.1.call-done = bf16[2048,1024]{1,0:T(8,128)(2,1)} async-done(((bf16[128,1024]{1,0:T(8,128)(2,1)}), bf16[2048,1024]{1,0:T(8,128)(2,1)}) %all-gather.16.cloned.1.call-update) | async-done | bytes 4194320 | tf_op jit(solution)/shard_map/all_gather | solution.py:234
  285.3 17.4 %fusion.37 = (bf16[1024,1024]{1,0:T(8,128)(2,1)S(1)}, f32[1024,1024]{1,0:T(8,128)}) fusion(f32[1024]{0:T(1024)S(1)} %copy-done.43, bf16[1024,2048]{1,0:T(8,128)(2,1)} %all-gather.14.cloned.1.call-done, bf16[2048,1024]{1,0:T(8,128)(2,1)} %all-gather.16.cloned.1.call-done), kind=kOutput, calls=%fused_computation.57 | convolution fusion | flops 4364173312 | bytes 14684160 | tf_op jit(solution)/shard_map/dot_general | solution.py:256
  304.1 6.3 convolution_convert_fusion.1
  310.3 6.4 copy.103
  316.8 38.2 %reduce-scatter.22.cloned.1.call-done = bf16[128,256]{1,0:T(8,128)(2,1)} async-done(((bf16[2048,256]{1,0:T(8,128)(2,1)}), bf16[128,256]{1,0:T(8,128)(2,1)}) %reduce-scatter.22.cloned.1.call-update) | async-done | bytes 65552
  356.9 82.2 %reduce-scatter.24.cloned.1.call-done = bf16[128,1024]{1,0:T(8,128)(2,1)} async-done(((bf16[2048,1024]{1,0:T(8,128)(2,1)}), bf16[128,1024]{1,0:T(8,128)(2,1)}) %reduce-scatter.24.cloned.1.call-update) | async-done | bytes 262160
  442.4 43.5 %all-gather.12.cloned.1.call-done = bf16[256,2048]{1,0:T(8,128)(2,1)} async-done(((bf16[256,128]{1,0:T(8,128)(2,1)}), bf16[256,2048]{1,0:T(8,128)(2,1)}) %all-gather.12.cloned.1.call-update) | async-done | bytes 1048592 | tf_op jit(solution)/shard_map/all_gather | solution.py:233
  485.9 4.6 convolution_convert_fusion.5
  490.5 23.7 %while.31 = (s32[]{:T(128)}, f32[1024,1,256]{0,2,1:T(8,128)}, f32[1024,1,256]{0,2,1:T(8,128)}, f32[2,512,1,256]{3,1,2,0:T(8,128)}, bf16[2,512,1,256]{3,1,2,0:T(8...) while((s32[]{:T(128)}, f32[1024,1,256]{0,2,1:T(8,128)}, ...), condition=%wide.region_12.13_spmd.clone.clone, body=%wide.region_10.12_spmd.clone.sunk.clone | while | flops 1349910016 | bytes 31484124 | solution.py:154
  490.5 1.6 fusion.200
  492.1 2.2 multiply_reduce_fusion.3
  494.6 2.5 fusion.201
  497.1 2.4 fusion.202
  503.6 2.2 multiply_reduce_fusion.3
  506.1 2.9 fusion.201
  509.0 2.8 fusion.202
  517.0 2.1 slice.108
  524.4 4.9 fusion.54
  529.6 7.9 convolution_convert_fusion
  537.5 9.1 all-gather.18.cloned.1.call-done
  546.6 10.3 %fusion.128 = (f32[1024]{0:T(1024)}, bf16[1024,1024]{1,0:T(8,128)(2,1)S(1)}) fusion(f32[1024,1024]{1,0:T(8,128)} %get-tuple-element.410, f32[1024]{0:T(1024)S(1)} %copy-done.43, bf16[1024,2048]{1,0:T(8,128)(2,1)} %all-gather.20.cloned.1.call-done, bf16[1024,2048]{1,0:T(8,128)(2,1)} %all-gather.18.cloned.1.call-done), kind=kOutput, calls=%fused_computation.225 | convolution fusion | flops 4307549184 | bytes 14688256 | tf_op jit(solution)/shard_map/dot_general | solution.py:71
  558.2 6.1 convolution_convert_fusion.3
  564.4 7.2 fusion.133
  571.7 3.4 add_convert_fusion
  575.3 9.4 convolution_convert_fusion.2
  588.9 35.3 %reduce-scatter.18.cloned.1.call-done = bf16[128,3,256]{2,0,1:T(8,128)(2,1)} async-done(((bf16[2048,3,256]{2,0,1:T(8,128)(2,1)}), bf16[128,3,256]{2,0,1:T(8,128)(2,1)}) %reduce-scatter.18.cloned.1.call-update) | async-done | bytes 196624 | tf_op jit(solution)/shard_map/reduce_scatter | solution.py:335
  624.2 2.4 multiply_subtract_fusion.2
  628.0 50.5 %reduce-scatter.14.cloned.1.call-done = bf16[128,2048]{1,0:T(8,128)(2,1)} async-done(((bf16[1024,2048]{1,0:T(8,128)(2,1)}), bf16[128,2048]{1,0:T(8,128)(2,1)}) %reduce-scatter.14.cloned.1.call-update) | async-done | bytes 524304 | tf_op jit(solution)/shard_map/reduce_scatter | solution.py:305
  678.4 54.2 %reduce-scatter.16.cloned.1.call-done = bf16[128,2048]{1,0:T(8,128)(2,1)} async-done(((bf16[1024,2048]{1,0:T(8,128)(2,1)}), bf16[128,2048]{1,0:T(8,128)(2,1)}) %reduce-scatter.16.cloned.1.call-update) | async-done | bytes 524304 | tf_op jit(solution)/shard_map/reduce_scatter | solution.py:308
  732.6 2.0 fusion.82
  735.4 51.5 %reduce-scatter.12.cloned.1.call-done = bf16[128,2048]{1,0:T(8,128)(2,1)} async-done(((bf16[1024,2048]{1,0:T(8,128)(2,1)}), bf16[128,2048]{1,0:T(8,128)(2,1)}) %reduce-scatter.12.cloned.1.call-update) | async-done | bytes 524304 | tf_op jit(solution)/shard_map/reduce_scatter | solution.py:258
  786.9 3.4 convert_reduce_fusion.3
  790.9 79.2 %reduce-scatter.20.cloned.1.call-done = bf16[128,1024]{1,0:T(8,128)(2,1)} async-done(((bf16[2048,1024]{1,0:T(8,128)(2,1)}), bf16[128,1024]{1,0:T(8,128)(2,1)}) %reduce-scatter.20.cloned.1.call-update) | async-done | bytes 262160 | tf_op jit(solution)/shard_map/reduce_scatter | solution.py:341
  870.1 2.3 multiply_subtract_fusion.1
  872.5 142.2 %all-reduce.3.cloned.1.call-done = (f32[3,2048]{1,0:T(4,128)}, f32[8192]{0:T(1024)}, f32[2,2048]{1,0:T(2,128)}, f32[4,2048]{1,0:T(4,128)}) async-done(((f32[3,2048]{1,0:T(4,128)}, f32[8192]{0:T(1024)}, f32[2,2048]{1,0:T(2,128)}, f32[4,2048]{1,0:T(4,128)}), (f32[3,2048]{1,0:T(4,128)}, f32[8192]{0:T(1024)}, f32[2,2048]{1,0:T(2,128)}, f32[4,2048]{1,0:T(4,128)})) %all-reduce.3.cloned.1.call-update) | async-done | bytes 106512 | tf_op jit(solution)/shard_map/psum | solution.py:329
  (227 shorter events, 53.6 us)
Async XLA Ops:
  7.2 113.9 %copy-start.39 = (f32[3,256]{1,0:T(4,128)S(1)}, f32[3,256]{1,0:T(4,128)}, u32[]{:S(2)}) copy-start(f32[3,256]{1,0:T(4,128)} %param.38) | copy-start | bytes 9220
  7.2 60.5 %all-gather.10.cloned.1.call-start = ((), (), s32[]{:S(2)}) async-start(), calls=%async_computation.8 | async-start | bytes 3342336 | tf_op jit(solution)/shard_map/all_gather | solution.py:232
  9.2 111.9 %all-gather.8.cloned.1.call-start = ((), (), s32[]{:S(2)}) async-start(), calls=%async_computation.7 | async-start | bytes 4718592 | tf_op jit(solution)/shard_map/all_gather | solution.py:241
  16.7 157.4 %all-gather.20.cloned.1.call-start = ((), (), s32[]{:S(2)}) async-start(), calls=%async_computation.14 | async-start | bytes 4718592 | tf_op jit(solution)/shard_map/all_gather | solution.py:275
  17.5 210.1 %all-gather.14.cloned.1.call-start = ((), (), s32[]{:S(2)}) async-start(), calls=%async_computation.10 | async-start | bytes 4718592 | tf_op jit(solution)/shard_map/all_gather | solution.py:242
  18.1 267.3 %all-gather.16.cloned.1.call-start = ((), (), s32[]{:S(2)}) async-start(), calls=%async_computation.11 | async-start | bytes 4456448 | tf_op jit(solution)/shard_map/all_gather | solution.py:234
  18.9 336.2 %reduce-scatter.22.cloned.1.call-start = ((), (), s32[]{:S(2)}) async-start(), calls=%async_computation.19 | async-start | bytes 1114112
  145.1 33.9 %copy-start.7 = (bf16[2,512,1,256]{3,1,2,0:T(8,128)(2,1)}, bf16[2,512,1,256]{3,1,2,0:T(8,128)(2,1)S(1)}, u32[]{:S(2)}) copy-start(bf16[2,512,1,256]{3,1,2,0:T(8,128)(2,1)S(1)} %get-tuple-element.148) | copy-start | bytes 1572868
  174.1 111.2 %copy-start.43 = (f32[1024]{0:T(1024)S(1)}, f32[1024]{0:T(1024)}, u32[]{:S(2)}) copy-start(f32[1024]{0:T(1024)} %param.39) | copy-start | bytes 12292
  178.9 260.2 %reduce-scatter.24.cloned.1.call-start = ((), (), s32[]{:S(2)}) async-start(), calls=%async_computation.20 | async-start | bytes 4456448
  316.7 39.3 %copy-start.24 = (f32[256,128]{1,0:T(8,128)S(1)}, f32[256,128]{1,0:T(8,128)}, u32[]{:S(2)}) copy-start(f32[256,128]{1,0:T(8,128)} %param.35) | copy-start | bytes 393220
  316.7 39.3 %copy-start.25 = (f32[256,128]{1,0:T(8,128)S(1)}, f32[256,128]{1,0:T(8,128)}, u32[]{:S(2)}) copy-start(f32[256,128]{1,0:T(8,128)} %param.45) | copy-start | bytes 393220
  316.7 39.3 %copy-start.26 = (f32[256,128]{1,0:T(8,128)S(1)}, f32[256,128]{1,0:T(8,128)}, u32[]{:S(2)}) copy-start(f32[256,128]{1,0:T(8,128)} %param.44) | copy-start | bytes 393220
  316.7 123.6 %copy-start.15 = (f32[1024,128]{1,0:T(8,128)S(1)}, f32[1024,128]{1,0:T(8,128)}, u32[]{:S(2)}) copy-start(f32[1024,128]{1,0:T(8,128)} %param.37) | copy-start | bytes 1572868
  316.7 123.6 %copy-start.16 = (f32[1024,128]{1,0:T(8,128)S(1)}, f32[1024,128]{1,0:T(8,128)}, u32[]{:S(2)}) copy-start(f32[1024,128]{1,0:T(8,128)} %param.49) | copy-start | bytes 1572868
  316.7 123.6 %copy-start.17 = (f32[1024,128]{1,0:T(8,128)S(1)}, f32[1024,128]{1,0:T(8,128)}, u32[]{:S(2)}) copy-start(f32[1024,128]{1,0:T(8,128)} %param.48) | copy-start | bytes 1572868
  316.8 169.1 %all-gather.12.cloned.1.call-start = ((), (), s32[]{:S(2)}) async-start(), calls=%async_computation.9 | async-start | bytes 1114112 | tf_op jit(solution)/shard_map/all_gather | solution.py:233
  356.9 189.7 %all-gather.18.cloned.1.call-start = ((), (), s32[]{:S(2)}) async-start(), calls=%async_computation.12 | async-start | bytes 4456448 | tf_op jit(solution)/shard_map/all_gather | solution.py:235
  441.8 182.4 %reduce-scatter.18.cloned.1.call-start = ((), (), s32[]{:S(2)}) async-start(), calls=%async_computation.17 | async-start | bytes 3342336 | tf_op jit(solution)/shard_map/reduce_scatter | solution.py:335
  529.3 149.1 %reduce-scatter.14.cloned.1.call-start = ((), (), s32[]{:S(2)}) async-start(), calls=%async_computation.15 | async-start | bytes 4718592 | tf_op jit(solution)/shard_map/reduce_scatter | solution.py:305
  537.4 195.2 %reduce-scatter.16.cloned.1.call-start = ((), (), s32[]{:S(2)}) async-start(), calls=%async_computation.16 | async-start | bytes 4718592 | tf_op jit(solution)/shard_map/reduce_scatter | solution.py:308
  564.4 222.5 %reduce-scatter.12.cloned.1.call-start = ((), (), s32[]{:S(2)}) async-start(), calls=%async_computation.13 | async-start | bytes 4718592 | tf_op jit(solution)/shard_map/reduce_scatter | solution.py:258
  575.1 295.0 %reduce-scatter.20.cloned.1.call-start = ((), (), s32[]{:S(2)}) async-start(), calls=%async_computation.18 | async-start | bytes 4456448 | tf_op jit(solution)/shard_map/reduce_scatter | solution.py:341
  584.8 39.4 %copy-start.12 = (f32[128,3,256]{2,0,1:T(8,128)S(1)}, f32[128,3,256]{2,0,1:T(8,128)}, u32[]{:S(2)}) copy-start(f32[128,3,256]{2,0,1:T(8,128)} %param.34) | copy-start | bytes 1179652
  584.8 147.8 %copy-start.2 = (bf16[128,2048]{1,0:T(8,128)(2,1)S(1)}, bf16[128,2048]{1,0:T(8,128)(2,1)}, u32[]{:S(2)}) copy-start(bf16[128,2048]{1,0:T(8,128)(2,1)} %param.31) | copy-start | bytes 1572868
  584.8 147.8 %copy-start.21 = (f32[1,2048]{1,0:T(1,128)S(1)}, f32[1,2048]{1,0:T(1,128)}, u32[]{:S(2)}) copy-start(f32[1,2048]{1,0:T(1,128)} %copy-done.20) | copy-start | bytes 24580
  584.8 147.8 %copy-start.23 = (f32[1,2048]{1,0:T(1,128)S(1)}, f32[1,2048]{1,0:T(1,128)}, u32[]{:S(2)}) copy-start(f32[1,2048]{1,0:T(1,128)} %copy-done.22) | copy-start | bytes 24580
  584.8 202.1 %copy-start.11 = (bf16[128,2048]{1,0:T(8,128)(2,1)S(1)}, bf16[128,2048]{1,0:T(8,128)(2,1)}, u32[]{:S(2)}) copy-start(bf16[128,2048]{1,0:T(8,128)(2,1)} %param.32) | copy-start | bytes 1572868
  584.8 429.9 %all-reduce.3.cloned.1.call-start = ((), (), s32[]{:S(2)}) async-start(), calls=%async_computation.21 | async-start | bytes 229376 | tf_op jit(solution)/shard_map/psum | solution.py:329
  587.5 199.4 %copy-start.29 = (f32[1,2048]{1,0:T(1,128)S(1)}, f32[1,2048]{1,0:T(1,128)}, u32[]{:S(2)}) copy-start(f32[1,2048]{1,0:T(1,128)} %get-tuple-element.403) | copy-start | bytes 24580
  587.5 199.4 %copy-start.30 = (f32[1,2048]{1,0:T(1,128)S(1)}, f32[1,2048]{1,0:T(1,128)}, u32[]{:S(2)}) copy-start(f32[1,2048]{1,0:T(1,128)} %get-tuple-element.406) | copy-start | bytes 24580
  587.5 199.4 %copy-start.36 = (f32[128]{0:T(128)S(1)}, f32[128]{0:T(128)}, u32[]{:S(2)}) copy-start(f32[128]{0:T(128)} %copy-done.35) | copy-start | bytes 1540
  587.5 199.4 %copy-start.38 = (f32[128]{0:T(128)S(1)}, f32[128]{0:T(128)}, u32[]{:S(2)}) copy-start(f32[128]{0:T(128)} %copy-done.37) | copy-start | bytes 1540
  588.9 281.2 %copy-start.10 = (f32[128,1024]{1,0:T(8,128)S(1)}, f32[128,1024]{1,0:T(8,128)}, u32[]{:S(2)}) copy-start(f32[128,1024]{1,0:T(8,128)} %param.36) | copy-start | bytes 1572868
  588.9 281.2 %copy-start.18 = (f32[128,1024]{1,0:T(8,128)S(1)}, f32[128,1024]{1,0:T(8,128)}, u32[]{:S(2)}) copy-start(f32[128,1024]{1,0:T(8,128)} %param.47) | copy-start | bytes 1572868
  588.9 281.2 %copy-start.19 = (f32[128,1024]{1,0:T(8,128)S(1)}, f32[128,1024]{1,0:T(8,128)}, u32[]{:S(2)}) copy-start(f32[128,1024]{1,0:T(8,128)} %param.46) | copy-start | bytes 1572868
  734.6 280.1 %copy-start.28 = (f32[2,2048]{1,0:T(2,128)S(1)}, f32[2,2048]{1,0:T(2,128)}, u32[]{:S(2)}) copy-start(f32[2,2048]{1,0:T(2,128)} %param.40) | copy-start | bytes 49156
  734.6 280.1 %copy-start.33 = (f32[2,2048]{1,0:T(2,128)S(1)}, f32[2,2048]{1,0:T(2,128)}, u32[]{:S(2)}) copy-start(f32[2,2048]{1,0:T(2,128)} %param.55) | copy-start | bytes 49156
  734.6 280.0 %copy-start.34 = (f32[2,2048]{1,0:T(2,128)S(1)}, f32[2,2048]{1,0:T(2,128)}, u32[]{:S(2)}) copy-start(f32[2,2048]{1,0:T(2,128)} %param.54) | copy-start | bytes 49156
  734.6 281.4 %copy-start.27 = (f32[4,2048]{1,0:T(4,128)S(1)}, f32[4,2048]{1,0:T(4,128)}, u32[]{:S(2)}) copy-start(f32[4,2048]{1,0:T(4,128)} %param.41) | copy-start | bytes 98308
  734.7 281.4 %copy-start.31 = (f32[4,2048]{1,0:T(4,128)S(1)}, f32[4,2048]{1,0:T(4,128)}, u32[]{:S(2)}) copy-start(f32[4,2048]{1,0:T(4,128)} %param.57) | copy-start | bytes 98308
  734.7 281.4 %copy-start.32 = (f32[4,2048]{1,0:T(4,128)S(1)}, f32[4,2048]{1,0:T(4,128)}, u32[]{:S(2)}) copy-start(f32[4,2048]{1,0:T(4,128)} %param.56) | copy-start | bytes 98308
  734.7 282.8 %copy-start.40 = (f32[3,256]{1,0:T(4,128)S(1)}, f32[3,256]{1,0:T(4,128)}, u32[]{:S(2)}) copy-start(f32[3,256]{1,0:T(4,128)} %param.38) | copy-start | bytes 9220
  734.7 282.8 %copy-start.41 = (f32[3,256]{1,0:T(4,128)S(1)}, f32[3,256]{1,0:T(4,128)}, u32[]{:S(2)}) copy-start(f32[3,256]{1,0:T(4,128)} %param.51) | copy-start | bytes 9220
  734.7 282.8 %copy-start.42 = (f32[3,256]{1,0:T(4,128)S(1)}, f32[3,256]{1,0:T(4,128)}, u32[]{:S(2)}) copy-start(f32[3,256]{1,0:T(4,128)} %param.50) | copy-start | bytes 9220
  734.7 284.1 %copy-start.44 = (f32[1024]{0:T(1024)S(1)}, f32[1024]{0:T(1024)}, u32[]{:S(2)}) copy-start(f32[1024]{0:T(1024)} %param.39) | copy-start | bytes 12292
  734.7 284.1 %copy-start.45 = (f32[1024]{0:T(1024)S(1)}, f32[1024]{0:T(1024)}, u32[]{:S(2)}) copy-start(f32[1024]{0:T(1024)} %param.53) | copy-start | bytes 12292
  734.7 284.1 %copy-start.46 = (f32[1024]{0:T(1024)S(1)}, f32[1024]{0:T(1024)}, u32[]{:S(2)}) copy-start(f32[1024]{0:T(1024)} %param.52) | copy-start | bytes 12292
  (23 other events, 116.0 us)
Sparse Core Ops, SparseCore 0:
  10.9 56.7 all-gather.9
  69.9 51.1 all-gather.7
  122.7 51.3 all-gather.19
  176.2 51.3 all-gather.13
  230.4 54.8 all-gather.15
  289.6 65.4 reduce-scatter.21
  359.6 79.4 reduce-scatter.23
  442.0 43.8 all-gather.11
  488.8 57.8 all-gather.17
  550.5 73.6 reduce-scatter.17
  626.6 51.7 reduce-scatter.13
  680.7 51.8 reduce-scatter.15
  735.0 51.8 reduce-scatter.11
  790.8 79.2 reduce-scatter.19
  877.4 137.1 all-reduce.2
where the time goes:
time: 1040 us; the launch traced here: 1030 us
  waiting for transfers between devices  824 us (79%)
  matrix products  117 us (11%)
  other arithmetic  35.1 us (3%)
  local copies, waits for them, and re-layouts  33.7 us (3%)
  between operations  15 us (1%)
    psum x1, waiting for transfers between devices, local(): lax.psum((gain_part, bias_part, qkv_bias_all, up_bias_all), ('dp', 'tenso...  142 us
    unnamed x17, waiting for transfers between devices  122 us
    reduce_scatter x1, waiting for transfers between devices, local(): lax.psum_scatter(up_grad.astype(jnp.bfloat16), 'dp', scatter_dimension=0,...  79.2 us
    all_gather x1, waiting for transfers between devices, local(): lax.all_gather(sent[2], 'dp', axis=0, tiled=True)  57.7 us
    reduce_scatter x1, waiting for transfers between devices, local(): lax.psum_scatter(second_part.astype(jnp.bfloat16), 'tensor', scatter_dime...  54.2 us
    all_gather x1, waiting for transfers between devices, local(): lax.all_gather(first_local, 'tensor', axis=0, tiled=True)  53.4 us
    reduce_scatter x1, waiting for transfers between devices, local(): lax.psum_scatter((jnp.dot(mixed_low, out_full, preferred_element_type=jnp...  51.5 us
    reduce_scatter x1, waiting for transfers between devices, local(): lax.psum_scatter(first_part.astype(jnp.bfloat16), 'tensor', scatter_dimen...  50.5 us
  transfers between devices with their start and end apart: 15, of which 15 were waited for; matrix products, arithmetic and copies ran while one was open for 17% of the time, Pallas kernels for 0%

commit v1 on v0

v1 whole, which is shorter than its diff:
```python
import functools
import math

import jax
import jax.numpy as jnp
from jax import lax
from jax.experimental import pallas as pl
from jax.experimental.pallas import tpu as pltpu
from jax.sharding import PartitionSpec as P

F32 = jnp.float32
BF16 = jnp.bfloat16
MESH = pl.DeviceIdType.MESH

D = 2048
HEAD = 256
QKV = 3 * HEAD
UNITS = 1024
WIDE = QKV + UNITS
DEEP = HEAD + UNITS
TOK = 1024
OWN = 128
TILE = 512
QROWS = 256
ROT = 64
STEP = 10

NORM_EPS = 1e-05
BETA_ONE = 0.9
BETA_TWO = 0.95
ADAM_EPS = 1e-08
STEP_RATES = (0.04, 0.2, 0.04, 0.02, 0.3, 0.3, 0.5, 0.3)
DECAY_RATES = (0.01, 0.01, 0.01, 0.01, 0.0, 0.0, 0.0, 0.0)


def place():
    dp = lax.axis_index("dp")
    tensor = lax.axis_index("tensor")
    return (
        lax.div(dp, 8),
        lax.rem(lax.div(dp, 2), 4),
        lax.rem(dp, 2),
        lax.div(tensor, 4),
        lax.rem(tensor, 4),
    )


def device(zh, y, core, zl, x):
    return ((zh * 4 + y) * 2 + core, zl * 4 + x)


def around(pos, step):
    return lax.rem(pos + step + 4, 4)


def neighbours(spot):
    zh, y, core, zl, x = spot
    return {
        "x+": device(zh, y, core, zl, around(x, 1)),
        "x-": device(zh, y, core, zl, around(x, -1)),
        "y+": device(zh, around(y, 1), core, zl, x),
        "y-": device(zh, around(y, -1), core, zl, x),
        "zl": device(zh, y, core, 1 - zl, x),
        "zh": device(1 - zh, y, core, zl, x),
        "core": device(zh, y, 1 - core, zl, x),
    }


class Links:
    def __init__(self, send_sems, recv_sems):
        self.send_sems, self.recv_sems = send_sems, recv_sems
        self.copies = []

    def send(self, src, dst, target):
        index = len(self.copies)
        copy = pltpu.make_async_remote_copy(
            src_ref=src,
            dst_ref=dst,
            send_sem=self.send_sems.at[index],
            recv_sem=self.recv_sems.at[index],
            device_id=target,
            device_id_type=MESH,
        )
        copy.start()
        self.copies.append(copy)
        return copy

    def drain(self):
        for copy in self.copies:
            copy.wait_send()


class Gather:
    def __init__(self, links, block, z, ring, z_dev, plus, minus, core=None):
        self.links, self.block, self.z, self.ring = links, block, z, ring
        self.z_dev, self.plus, self.minus, self.core = z_dev, plus, minus, core
        self.core_copies = []

    def pass_on(self, z, ring, half=None):
        if self.core is not None:
            part = self.block(z, ring, half)
            self.core_copies.append(self.links.send(part, part, self.core))

    def to(self, z, ring, half, target):
        part = self.block(z, ring, half)
        return self.links.send(part, part, target)

    def start(self):
        self.by_z = self.to(self.z, self.ring, None, self.z_dev)
        self.first = (
            self.to(self.z, self.ring, None, self.plus),
            self.to(self.z, self.ring, None, self.minus),
        )
        self.pass_on(self.z, self.ring)

    def partner(self):
        self.by_z.wait_recv()
        self.second = (
            self.to(1 - self.z, self.ring, None, self.plus),
            self.to(1 - self.z, self.ring, None, self.minus),
        )
        self.pass_on(1 - self.z, self.ring)

    def forward(self, z, copies):
        copies[0].wait_recv()
        up = self.to(z, around(self.ring, -1), 0, self.plus)
        copies[1].wait_recv()
        down = self.to(z, around(self.ring, 1), 1, self.minus)
        self.pass_on(z, around(self.ring, -1))
        self.pass_on(z, around(self.ring, 1))
        return (up, down)

    def near(self):
        self.third = self.forward(self.z, self.first)

    def far(self):
        self.fourth = self.forward(1 - self.z, self.second)

    def last(self):
        for z, copies in ((self.z, self.third), (1 - self.z, self.fourth)):
            copies[0].wait_recv()
            copies[1].wait_recv()
            self.pass_on(z, around(self.ring, 2))

    def finish(self):
        for copy in self.core_copies:
            copy.wait_recv()


def rows_of(ref, start, count):
    return ref.at[pl.ds(pl.multiple_of(start, 16), count)]


def gelu_parts(pre):
    cdf = 0.5 * (1.0 + lax.erf(pre * (1.0 / math.sqrt(2.0))))
    density = jnp.exp(-0.5 * pre * pre) * (1.0 / math.sqrt(2.0 * math.pi))
    return pre * cdf, cdf + pre * density


def spin(rows, cosines, sines, back):
    low = rows[:, :128]
    lane = lax.broadcasted_iota(jnp.int32, low.shape, 1)
    ahead = pltpu.roll(low, 96, 1)
    behind = pltpu.roll(low, 32, 1)
    turned = jnp.where(lane < 32, -ahead, jnp.where(lane < 64, behind, 0.0))
    if back:
        turned = -turned
    return jnp.concatenate([low * cosines + turned * sines, rows[:, 128:]], axis=1)


def forward_kernel(
    lens,
    x_in,
    cot_in,
    w_qkv,
    w_out,
    w_up,
    w_down,
    b_qkv,
    b_up,
    gains,
    biases,
    unit_out,
    cot_out,
    wide_out,
    deep_out,
    q_out,
    k_out,
    v_out,
    acts_out,
    slope_out,
    probs_out,
    turn_out,
    branch_out,
    unit,
    cot,
    wide,
    deep,
    q,
    k,
    v,
    acts,
    slope,
    probs,
    turn,
    branch,
    begins,
    normed,
    send_sems,
    recv_sems,
    out_sems,
):
    spot = place()
    zh, y, core, zl, x = spot
    near = neighbours(spot)
    barrier = pltpu.get_barrier_semaphore()
    for target in near.values():
        pl.semaphore_signal(barrier, inc=1, device_id=target, device_id_type=MESH)

    links = Links(send_sems, recv_sems)
    stores = []

    def store(src, dst):
        copy = pltpu.make_async_copy(src, dst, out_sems.at[len(stores)])
        copy.start()
        stores.append(copy)

    def token_block(ref):
        def block(z, ring, half):
            start = (z * 4 + ring) * OWN
            if half is None:
                return rows_of(ref, start, OWN)
            return rows_of(ref, start + half * (OWN // 2), OWN // 2)

        return block

    def wide_block(z, ring, half):
        start = ((z * 4 + ring) * 2 + core) * OWN
        if half is None:
            return rows_of(wide, start, OWN)
        return rows_of(wide, start + half * (OWN // 2), OWN // 2)

    def deep_block(z, ring, half):
        columns = pl.ds(pl.multiple_of(((z * 4 + ring) * 2 + core) * OWN, OWN), OWN)
        if half is None:
            return deep.at[:, columns]
        return deep.at[pl.ds(half * (DEEP // 2), DEEP // 2), columns]

    tensor_ends = (zl, x, near["zl"], near["x+"], near["x-"])
    data_ends = (zh, y, near["zh"], near["y+"], near["y-"], near["core"])
    units = Gather(links, token_block(unit), *tensor_ends)
    grads = Gather(links, token_block(cot), *tensor_ends)
    wides = Gather(links, wide_block, *data_ends)
    deeps = Gather(links, deep_block, *data_ends)

    rows = x_in[...].astype(F32)
    centred = rows - jnp.mean(rows, axis=-1, keepdims=True)
    variance = jnp.mean(centred * centred, axis=-1, keepdims=True)
    mine = pl.ds(pl.multiple_of((zl * 4 + x) * OWN, OWN), OWN)
    unit[mine, :] = (centred * lax.rsqrt(variance + NORM_EPS)).astype(BF16)
    own = pl.ds(pl.multiple_of(((zh * 4 + y) * 2 + core) * OWN, OWN), OWN)
    wide[own, :QKV] = w_qkv[...].astype(BF16)
    wide[own, QKV:] = w_up[...].astype(BF16)
    pl.semaphore_wait(barrier, len(near))
    units.start()
    wides.start()
    cot[mine, :] = cot_in[...]
    deep[:HEAD, own] = w_out[...].astype(BF16)
    deep[HEAD:, own] = w_down[...].astype(BF16)

    index = lax.broadcasted_iota(jnp.int32, (TOK, 128), 0)
    ends = [lens[0, 0]]
    for seq in range(1, 3):
        ends.append(ends[-1] + lens[0, seq])
    begin = jnp.zeros((TOK, 128), jnp.int32)
    for end in ends:
        begin = jnp.where(index >= end, end, begin)
    begins[...] = begin
    lane = lax.broadcasted_iota(jnp.int32, (TOK, 128), 1)
    rate = jnp.exp(lax.rem(lane, 32).astype(F32) * (-2.0 * math.log(10000.0) / ROT))
    angle = (index - begin).astype(F32) * rate
    turn[0] = jnp.where(lane < ROT, jnp.cos(angle), 1.0)
    turn[1] = jnp.where(lane < ROT, jnp.sin(angle), 0.0)
    store(turn, turn_out)

    units.partner()
    wides.partner()
    wides.near()
    units.near()
    wides.far()
    units.far()
    deeps.start()
    grads.start()
    wides.last()
    units.last()
    wides.finish()
    units.finish()
    grads.partner()
    deeps.partner()
    store(unit, unit_out)
    store(wide, wide_out)

    def project(tile, _):
        part = pl.ds(pl.multiple_of(tile * TILE, TILE), TILE)
        unit_rows = unit[part, :].astype(F32)
        normed[0] = (unit_rows * gains[0:1, :] + biases[0:1, :]).astype(BF16)
        normed[1] = (unit_rows * gains[1:2, :] + biases[1:2, :]).astype(BF16)
        cosines, sines = turn[0, part, :], turn[1, part, :]
        for which, target in enumerate((q, k, v)):
            columns = slice(which * HEAD, (which + 1) * HEAD)
            head = jnp.dot(normed[0], wide[:, columns], preferred_element_type=F32)
            head = head + b_qkv[which : which + 1, :]
            if which < 2:
                head = spin(head, cosines, sines, False)
            target[part, :] = head.astype(BF16)

        def hidden(piece, _):
            shift = pl.multiple_of(piece * 256, 256)
            pre = jnp.dot(normed[1], wide[:, pl.ds(QKV + shift, 256)], preferred_element_type=F32)
            pre = pre + b_up[0:1, pl.ds(shift, 256)]
            value, rise = gelu_parts(pre)
            acts[part, pl.ds(HEAD + shift, 256)] = value.astype(BF16)
            slope[part, pl.ds(shift, 256)] = rise.astype(BF16)
            return 0

        lax.fori_loop(0, UNITS // 256, hidden, 0)
        return 0

    project(0, 0)
    deeps.near()
    grads.near()
    project(1, 0)
    deeps.far()
    store(q, q_out)
    store(k, k_out)
    store(v, v_out)
    store(slope, slope_out)

    for block in range(TOK // QROWS):
        part = slice(block * QROWS, (block + 1) * QROWS)
        keys = (block + 1) * QROWS
        scores = lax.dot_general(
            q[part, :], k[:keys, :], (((1,), (1,)), ((), ())), preferred_element_type=F32
        ) * (HEAD**-0.5)
        key = lax.broadcasted_iota(jnp.int32, (QROWS, keys), 1)
        row = lax.broadcasted_iota(jnp.int32, (QROWS, keys), 0) + block * QROWS
        allowed = (key <= row) & (key >= begins[part, 0:1])
        scores = jnp.where(allowed, scores, -jnp.inf)
        expo = jnp.exp(scores - jnp.max(scores, axis=-1, keepdims=True))
        share = (expo / jnp.sum(expo, axis=-1, keepdims=True)).astype(BF16)
        probs[part, :keys] = share
        acts[part, :HEAD] = jnp.dot(share, v[:keys, :], preferred_element_type=F32).astype(BF16)
    store(probs, probs_out)
    store(acts, acts_out)
    grads.far()
    deeps.last()
    deeps.finish()
    store(deep, deep_out)

    def mix(tile, _):
        part = pl.ds(pl.multiple_of(tile * TILE, TILE), TILE)

        def piece(step, _):
            columns = pl.ds(pl.multiple_of(step * 256, 256), 256)
            branch[part, columns] = jnp.dot(
                acts[part, :], deep[:, columns], preferred_element_type=F32
            ).astype(BF16)
            return 0

        return lax.fori_loop(0, D // 256, piece, 0)

    lax.fori_loop(0, TOK // TILE, mix, 0)
    store(branch, branch_out)
    grads.last()
    store(cot, cot_out)
    for copy in stores:
        copy.wait()
    links.drain()


FORWARD_KEPT = (
    ((TOK, D), BF16),
    ((TOK, D), BF16),
    ((D, WIDE), BF16),
    ((DEEP, D), BF16),
    ((TOK, HEAD), BF16),
    ((TOK, HEAD), BF16),
    ((TOK, HEAD), BF16),
    ((TOK, DEEP), BF16),
    ((TOK, UNITS), BF16),
    ((TOK, TOK), BF16),
    ((2, TOK, 128), F32),
    ((TOK, D), BF16),
)


def run_forward(lens, *inputs):
    vmem = pl.BlockSpec(memory_space=pltpu.VMEM)
    return pl.pallas_call(
        forward_kernel,
        out_shape=[jax.ShapeDtypeStruct(*kept) for kept in FORWARD_KEPT],
        in_specs=[pl.BlockSpec(memory_space=pltpu.SMEM)] + [vmem] * len(inputs),
        out_specs=[pl.BlockSpec(memory_space=pl.ANY)] * len(FORWARD_KEPT),
        scratch_shapes=[pltpu.VMEM(*kept) for kept in FORWARD_KEPT]
        + [
            pltpu.VMEM((TOK, 128), jnp.int32),
            pltpu.VMEM((2, TILE, D), BF16),
            pltpu.SemaphoreType.DMA((64,)),
            pltpu.SemaphoreType.DMA((64,)),
            pltpu.SemaphoreType.DMA((len(FORWARD_KEPT),)),
        ],
        compiler_params=pltpu.CompilerParams(
            collective_id=0, has_side_effects=True, vmem_limit_bytes=60 * 2**20
        ),
        cost_estimate=pl.CostEstimate(flops=14 * 10**9, bytes_accessed=40 * 10**6, transcendentals=0),
        name="forward",
    )(lens, *inputs)


def over_rows(left, right):
    return lax.dot_general(left, right, (((0,), (0,)), ((), ())), preferred_element_type=F32)


def by_rows(left, right):
    return lax.dot_general(left, right, (((1,), (1,)), ((), ())), preferred_element_type=F32)


def adam_step(weight, gradient, moment_one, moment_two, step_rate, decay_rate):
    moment_one = BETA_ONE * moment_one + (1.0 - BETA_ONE) * gradient
    moment_two = BETA_TWO * moment_two + (1.0 - BETA_TWO) * gradient * gradient
    ratio = (
        moment_one
        / (1.0 - BETA_ONE**STEP)
        / (jnp.sqrt(moment_two / (1.0 - BETA_TWO**STEP)) + ADAM_EPS)
    )
    return (moment_one, moment_two, weight - step_rate * (ratio + decay_rate * weight))


def local(
    layer_in, cotangent, seq_lengths, w_qkv, w_out, w_up, w_down, b_qkv, b_up, norm_gains, row_biases,
    m_qkv, v_qkv, m_out, v_out, m_up, v_up, m_down, v_down, m_bqkv, v_bqkv, m_bup, v_bup,
    m_gains, v_gains, m_biases, v_biases,
):
    tensor_size = lax.axis_size("tensor")
    tensor_place = lax.axis_index("tensor")
    resid = layer_in.astype(F32)
    row_mean = jnp.mean(resid, axis=-1, keepdims=True)
    centered = resid - row_mean
    variance = jnp.mean(centered * centered, axis=-1, keepdims=True)
    inverse = lax.rsqrt(variance + NORM_EPS)
    own_unit = centered * inverse
    (unit, grad_rows, wide, deep, q, k, v, acts, slope, probs, turn, branch) = run_forward(
        seq_lengths, layer_in, cotangent, w_qkv.reshape(OWN, QKV), w_out, w_up, w_down,
        b_qkv, b_up.reshape(1, UNITS), norm_gains, row_biases)
    branch = lax.psum_scatter(branch, "tensor", scatter_dimension=0, tiled=True).astype(F32)
    out_rows = (resid + branch + row_biases[2] + row_biases[3]).astype(BF16)
    deep_grad = over_rows(acts, grad_rows)
    back = by_rows(grad_rows, deep)
    mixed_grad = back[:, :HEAD].astype(BF16)
    inner_grad = back[:, HEAD:] * slope.astype(F32)
    inner_low = inner_grad.astype(BF16)
    unit_f = unit.astype(F32)
    first_normed = (unit_f * norm_gains[0] + row_biases[0]).astype(BF16)
    second_normed = (unit_f * norm_gains[1] + row_biases[1]).astype(BF16)
    up_grad = over_rows(second_normed, inner_low)
    second_part = by_rows(inner_low, wide[:, QKV:])
    index = jnp.arange(TOK)
    pf = jnp.where(index[:, None] // QROWS >= index[None, :] // QROWS, probs.astype(F32), 0.0)
    prob_grad = by_rows(mixed_grad, v)
    delta = jnp.sum(pf * prob_grad, axis=-1, keepdims=True)
    score_grad = (pf * (prob_grad - delta)).astype(BF16)
    scale = HEAD**-0.5
    query_grad = jnp.dot(score_grad, k, preferred_element_type=F32) * scale
    key_grad = over_rows(score_grad, q) * scale
    value_grad = over_rows(pf.astype(BF16), mixed_grad)

    def back_spin(rows):
        cosines, sines = turn[0, :, :64], turn[1, :, :64]
        sined = rows[:, :64] * sines
        turned = jnp.concatenate([sined[:, 32:], -sined[:, :32]], axis=1)
        return jnp.concatenate([rows[:, :64] * cosines + turned, rows[:, 64:]], axis=1)

    projected_grad = jnp.concatenate([back_spin(query_grad), back_spin(key_grad), value_grad], axis=1)
    projected_low = projected_grad.astype(BF16)
    qkv_grad = over_rows(first_normed, projected_low)
    first_part = by_rows(projected_low, wide[:, :QKV])
    qkv_bias_grad = jnp.sum(projected_grad, axis=0).reshape(3, HEAD)
    up_bias_grad = jnp.sum(inner_grad, axis=0)
    grad_own = cotangent.astype(F32)
    out_bias_grad = jnp.sum(grad_own, axis=0)
    gain_part = jnp.stack([jnp.sum(first_part * unit_f, axis=0), jnp.sum(second_part * unit_f, axis=0)])
    shift_part = jnp.stack([jnp.sum(first_part, axis=0), jnp.sum(second_part, axis=0)])
    unit_grad = lax.psum_scatter(
        (first_part * norm_gains[0] + second_part * norm_gains[1]).astype(BF16),
        "tensor", scatter_dimension=0, tiled=True).astype(F32)
    unit_mean = jnp.mean(unit_grad, axis=-1, keepdims=True)
    unit_proj = jnp.mean(unit_grad * own_unit, axis=-1, keepdims=True)
    input_grad = grad_own + inverse * (unit_grad - unit_mean - own_unit * unit_proj)
    bias_part = jnp.concatenate([shift_part, out_bias_grad[None, :], out_bias_grad[None, :]], axis=0)
    gain_sum, bias_sum = lax.psum((gain_part, bias_part), ("dp", "tensor"))
    qkv_bias_sum, up_bias_sum = lax.psum((qkv_bias_grad, up_bias_grad), "dp")
    wide_grad = jnp.concatenate([qkv_grad, up_grad], axis=1).astype(BF16)
    wide_sum = lax.psum_scatter(wide_grad, "dp", scatter_dimension=0, tiled=True).astype(F32)
    deep_sum = lax.psum_scatter(deep_grad.astype(BF16), "dp", scatter_dimension=1, tiled=True).astype(F32)
    params = (w_qkv, w_out, w_up, w_down, b_qkv, b_up, norm_gains, row_biases)
    grad_list = (wide_sum[:, :QKV].reshape(OWN, 3, HEAD), deep_sum[:HEAD], wide_sum[:, QKV:], deep_sum[HEAD:],
                 qkv_bias_sum, up_bias_sum, gain_sum, bias_sum)
    moments = ((m_qkv, v_qkv), (m_out, v_out), (m_up, v_up), (m_down, v_down), (m_bqkv, v_bqkv),
               (m_bup, v_bup), (m_gains, v_gains), (m_biases, v_biases))
    updated = []
    for which in range(8):
        updated.extend(adam_step(params[which], grad_list[which], moments[which][0], moments[which][1],
                                 STEP_RATES[which], DECAY_RATES[which]))
    return (out_rows, input_grad, *updated)


def solution(mesh):
    rows = P(("dp", "tensor"), None)
    qkv, out, up, down = P("dp", None, "tensor"), P("tensor", "dp"), P("dp", "tensor"), P("tensor", "dp")
    bqkv, bup = P(None, "tensor"), P("tensor")
    params = (qkv, out, up, down, bqkv, bup, P(), P())
    moments = [spec for spec in params for _ in range(2)]
    return jax.shard_map(
        local,
        mesh=mesh,
        in_specs=(rows, rows, P("dp", None), *params, *moments),
        out_specs=(rows, rows, *[spec for spec in params for _ in range(3)]),
        check_vma=False,
    )
```

time: 1040 us -> 432 us (0.42)
  waiting for transfers between devices: 824 us -> 79.2 us
  blocking collectives: 0 us -> 108 us
  Pallas kernels: 0 us -> 89.8 us
  matrix products: 117 us -> 56.9 us
  local copies, waits for them, and re-layouts: 33.7 us -> 44.7 us
    all_gather x7 -> x0, waiting for transfers between devices: 289 us -> none  [the longest x1 57.7 us: local(): lax.all_gather(sent[2], 'dp', axis=0, tiled=True)]
    reduce_scatter x5 -> x2, waiting for transfers between devices: 271 us -> 54.2 us  [the longest x1 52.4 us: local(): lax.psum_scatter(branch, 'tensor', scatter_dimension=0, tiled=True)]
    psum x1 -> x0, waiting for transfers between devices: 142 us -> none  [local(): lax.psum((gain_part, bias_part, qkv_bias_all, up_bias_all), ('dp', 'tenso...]
    psum x0 -> x2, blocking collectives: none -> 108 us  [the longest x1 68.9 us: local(): gain_sum, bias_sum = lax.psum((gain_part, bias_part), ('dp', 'tensor'))]
    unnamed x17 -> x6, waiting for transfers between devices: 122 us -> 24.9 us
    pallas_call x0 -> x1, Pallas kernels: none -> 89.8 us  [run_forward(): pl.pallas_call(forward_kernel, out_shape=[jax.ShapeDtypeStruct(*kept) for...]
    dot_general x18 -> x1, matrix products: 64.4 us -> 2.7 us  [local(): query_grad = jnp.dot(score_grad, k, preferred_element_type=F32) * scale]
    unnamed x118 -> x105, local copies, waits for them, and re-layouts: 21.1 us -> 35.7 us
  transfers between devices with their start and end apart: 15 -> 4, of which waited for: 15 -> 3; matrix products, arithmetic and copies ran while one was open for 17% -> 23% of each run, Pallas kernels for 0% -> 0%
where the time goes in v1:
time: 432 us; the launch traced here: 427 us
  blocking collectives  108 us (25%)
  Pallas kernels  89.8 us (21%)
  waiting for transfers between devices  79.2 us (18%)
  matrix products  56.9 us (13%)
  local copies, waits for them, and re-layouts  44.7 us (10%)
  other arithmetic  32.9 us (8%)
  between operations  14.7 us (3%)
    pallas_call x1, Pallas kernels, run_forward(): pl.pallas_call(forward_kernel, out_shape=[jax.ShapeDtypeStruct(*kept) for...  89.8 us
    psum x1, blocking collectives, local(): gain_sum, bias_sum = lax.psum((gain_part, bias_part), ('dp', 'tensor'))  68.9 us
    reduce_scatter x1, waiting for transfers between devices, local(): lax.psum_scatter(branch, 'tensor', scatter_dimension=0, tiled=True)  52.4 us
    psum x1, blocking collectives, local(): qkv_bias_sum, up_bias_sum = lax.psum((qkv_bias_grad, up_bias_grad), 'dp')  39.6 us
    unnamed x105, local copies, waits for them, and re-layouts  35.7 us
    dot_general x5, matrix products, over_rows(): lax.dot_general(left, right, (((0,), (0,)), ((), ())), preferred_element_...  27.9 us
    dot_general x4, matrix products, by_rows(): lax.dot_general(left, right, (((1,), (1,)), ((), ())), preferred_element_...  26.3 us
    unnamed x6, waiting for transfers between devices  24.9 us
  transfers between devices with their start and end apart: 4, of which 3 were waited for; matrix products, arithmetic and copies ran while one was open for 23% of the time, Pallas kernels for 0%

profile of v1, /device:TPU:0, one launch (start us, length us, event | category | flops | bytes accessed | tf_op | source)
XLA Modules:
  0.0 426.8 jit_solution(10142461268181253968)
XLA Ops:
  7.2 1.2 copy.92
  8.4 0.9 copy.93.w_qkv
  9.3 89.8 %forward.1 = (bf16[1024,2048]{1,0:T(8,128)(2,1)}, bf16[1024,2048]{1,0:T(8,128)(2,1)}, bf16[2048,1792]{1,0:T(8,128)(2,1)}, bf16[1280,2048]{1,0:T(8,128)(2,1)}, bf...) custom-call(s32[1,4]{1,0:T(1,128)} %lens.1, ...), custom_call_target="tpu_custom_call" | custom-call | flops 14000000000 | bytes 40000000 | tf_op jit(solution)/shard_map/forward/pallas_call | solution.py:399
  99.2 10.0 %convolution_convert_fusion = bf16[1280,2048]{1,0:T(8,128)(2,1)} fusion(bf16[1024,1280]{1,0:T(8,128)(2,1)} %get-tuple-element.49, bf16[1024,2048]{1,0:T(8,128)(2,1)} %get-tuple-element.40), kind=kOutput, calls=%fused_computation.11 | convolution fusion | flops 5371330560 | bytes 12058624 | tf_op jit(solution)/shard_map/dot_general | solution.py:421
  109.2 7.8 %copy.117 = bf16[1280,2048]{0,1:T(8,128)(2,1)} copy(bf16[1280,2048]{1,0:T(8,128)(2,1)} %convolution_convert_fusion) | data formatting | bytes 10485760
  117.1 9.3 %fusion.76 = f32[1024,1280]{1,0:T(8,128)S(1)} fusion(bf16[1024,2048]{1,0:T(8,128)(2,1)} %get-tuple-element.40, bf16[1280,2048]{1,0:T(8,128)(2,1)} %get-tuple-element.41), kind=kOutput, calls=%fused_computation.125 | convolution fusion | flops 5368709120 | bytes 14680064 | tf_op jit(solution)/shard_map/dot_general | solution.py:425
  126.4 1.0 multiply_reduce_fusion
  127.5 1.1 multiply_convert_fusion
  128.8 1.4 copy-done.9
  130.9 1.0 copy-done.5
  132.2 1.2 copy.101
  133.4 2.7 convolution_multiply_fusion.1
  136.1 1.3 slice.107
  138.0 0.9 copy.100
  138.9 2.5 copy.99
  141.5 1.5 maximum_add_fusion
  143.0 0.9 copy.98
  143.9 1.0 constant_dynamic-update-slice_fusion.3
  144.8 1.2 constant_dynamic-update-slice_fusion.2
  146.0 1.0 constant_dynamic-update-slice_fusion.1
  147.1 2.2 fusion.32
  149.9 1.1 copy-done.10
  151.0 6.7 %fusion.13 = f32[1024,2048]{1,0:T(8,128)S(1)} fusion(bf16[2048,1792]{1,0:T(8,128)(2,1)} %get-tuple-element.46, bf16[1024,1024]{1,0:T(8,128)(2,1)S(1)} %copy-done.10, f32[1024,1280]{1,0:T(8,128)S(1)} %bitcast.38), kind=kOutput, calls=%fused_computation.19 | convolution fusion | flops 4298113024 | bytes 18874368 | tf_op jit(solution)/shard_map/dot_general | solution.py:425
  157.8 9.3 %fusion.62 = (f32[2048]{0:T(1024)}, f32[2048]{0:T(1024)}, bf16[1024,2048]{1,0:T(8,128)(2,1)}, f32[2048]{0:T(1024)}, f32[2048]{0:T(1024)}) fusion(bf16[1024,2048]{1,0:T(8,128)(2,1)S(1)} %copy-done.39, f32[1024,2048]{1,0:T(8,128)S(1)} %fusion.13, f32[2048]{0:T(1024)S(1)} %bitcast.51, f32[2048]{0:T(1024)S(1)} %bitcast.53, ...), kind=kOutput, calls=%fused_computation.119 | convolution fusion | flops 3245072384 | bytes 23117824 | tf_op jit(solution)/shard_map/dot_general | solution.py:425
  167.9 8.4 %fusion.20 = bf16[2048,768]{0,1:T(8,128)(2,1)} fusion(bf16[1024,2048]{1,0:T(8,128)(2,1)} %get-tuple-element.48, f32[2048]{0:T(1024)S(1)} %bitcast.56, f32[2048]{0:T(1024)S(1)} %bitcast.54, f32[1024,768]{0,1:T(8,128)} %copy-done.7), kind=kOutput, calls=%fused_computation.27 | convolution fusion | flops 3231973376 | bytes 10502144 | tf_op jit(solution)/shard_map/dot_general | solution.py:421
  176.3 6.5 %fusion.17 = bf16[2048,1024]{0,1:T(8,128)(2,1)} fusion(bf16[1024,2048]{1,0:T(8,128)(2,1)S(1)} %copy-done.40, f32[2048]{0:T(1024)S(1)} %bitcast.55, f32[2048]{0:T(1024)S(1)} %bitcast.52, bf16[1024,1024]{1,0:T(8,128)(2,1)S(1)} %copy-done.11, f32[1024,1280]{1,0:T(8,128)S(1)} %bitcast.40), kind=kOutput, calls=%fused_computation.26 | convolution fusion | flops 4308598784 | bytes 14696448 | tf_op jit(solution)/shard_map/dot_general | solution.py:421
  182.8 7.6 %pad_maximum_fusion = bf16[2048,1792]{0,1:T(8,128)(2,1)} fusion(bf16[2048,1024]{0,1:T(8,128)(2,1)} %fusion.17, bf16[2048,768]{0,1:T(8,128)(2,1)} %fusion.20), kind=kLoop, calls=%fused_computation.12 | loop fusion | flops 14680064 | bytes 14680064 | tf_op jit(solution)/shard_map/concatenate | solution.py:502
  190.4 10.0 %copy.115 = bf16[2048,1792]{1,0:T(8,128)(2,1)} copy(bf16[2048,1792]{0,1:T(8,128)(2,1)} %pad_maximum_fusion) | data formatting | bytes 14680064
  200.4 1.0 copy-done.16
  202.1 2.2 reduce_sum.113
  204.4 3.5 fusion.25
  207.9 39.6 %all-reduce.1 = (f32[3,256]{1,0:T(4,128)S(1)}, f32[1024]{0:T(1024)S(1)}) all-reduce(f32[3,256]{1,0:T(4,128)S(1)} %reshape.162, f32[1024]{0:T(1024)S(1)} %fusion.25), channel_id=1, replica_groups=mesh['dp'=16,'tensor'=8] {'dp'}, use_global_device_ids=true, to_apply=%region_10.11 | all-reduce | flops 1792 | bytes 14336 | tf_op jit(solution)/shard_map/psum | solution.py:501
  249.8 1.2 copy.118
  251.1 1.8 multiply_subtract_fusion.3
  253.0 2.5 multiply_subtract_fusion
  255.5 1.8 reduce-scatter.11.cloned.1.call-done
  257.3 1.4 convert_reduce_fusion
  258.8 52.4 %reduce-scatter.9.cloned.1.call-done = bf16[128,2048]{1,0:T(8,128)(2,1)} async-done(((bf16[1024,2048]{1,0:T(8,128)(2,1)}), bf16[128,2048]{1,0:T(8,128)(2,1)}) %reduce-scatter.9.cloned.1.call-update) | async-done | bytes 524304 | tf_op jit(solution)/shard_map/reduce_scatter | solution.py:455
  311.2 3.2 convert_reduce_fusion.2
  314.4 68.9 %all-reduce = (f32[2,2048]{1,0:T(2,128)S(1)}, f32[4,2048]{1,0:T(4,128)S(1)}) all-reduce(f32[2,2048]{1,0:T(2,128)S(1)} %pad_maximum_fusion.2, f32[4,2048]{1,0:T(4,128)S(1)} %pad_maximum_fusion.1), channel_id=1, replica_groups=mesh['dp'=16,'tensor'=8] {'dp','tensor'}, use_global_device_ids=true, to_apply=%region_15.16 | all-reduce | flops 12288 | bytes 98304 | tf_op jit(solution)/shard_map/psum | solution.py:500
  384.6 24.2 %reduce-scatter.13.cloned.1.call-done = bf16[128,1792]{1,0:T(8,128)(2,1)} async-done(((bf16[2048,1792]{1,0:T(8,128)(2,1)}), bf16[128,1792]{1,0:T(8,128)(2,1)}) %reduce-scatter.13.cloned.1.call-update) | async-done | bytes 458768
  408.8 1.3 copy.116
  410.2 0.9 copy.102
  411.1 1.4 multiply_subtract_fusion.1
  412.5 2.0 copy.111
  414.5 2.0 copy.110
  416.6 1.0 copy.109
  417.6 2.4 multiply_subtract_fusion.2
  (125 shorter events, 8.0 us)
Async XLA Ops:
  7.2 242.6 %reduce-scatter.15.cloned.1.call-start = ((), (), s32[]{:S(2)}) async-start(), calls=%async_computation.7 | async-start | bytes 5570560
  117.0 140.3 %reduce-scatter.11.cloned.1.call-start = ((), (), s32[]{:S(2)}) async-start(), calls=%async_computation.5 | async-start | bytes 4718592 | tf_op jit(solution)/shard_map/reduce_scatter | solution.py:493
  117.1 9.3 %copy-start.1 = (bf16[1024,1024]{1,0:T(8,128)(2,1)S(1)}, bf16[1024,1024]{1,0:T(8,128)(2,1)}, u32[]{:S(2)}) copy-start(bf16[1024,1024]{1,0:T(8,128)(2,1)} %get-tuple-element.39) | copy-start | bytes 6291460
  117.1 9.3 %copy-start.15 = (bf16[1024,256]{1,0:T(8,128)(2,1)S(1)}, bf16[1024,256]{1,0:T(8,128)(2,1)}, u32[]{:S(2)}) copy-start(bf16[1024,256]{1,0:T(8,128)(2,1)} %get-tuple-element.42) | copy-start | bytes 1572868
  126.4 2.3 copy-start.2
  127.5 2.7 copy-start.38
  128.7 1.4 copy-start.9
  130.9 1.0 copy-start.5
  133.4 4.0 copy-start.3
  133.4 4.0 copy-start.6
  136.1 1.8 copy-start.4
  141.3 5.7 %copy-start.8 = (f32[1024,192]{0,1:T(8,128)S(1)}, f32[1024,192]{0,1:T(8,128)}, u32[]{:S(2)}) copy-start(f32[1024,192]{0,1:T(8,128)} %copy.101) | copy-start | bytes 2359300
  147.0 2.5 slice-start
  147.1 2.2 copy-start.20
  147.1 2.8 slice-start.1
  147.1 3.8 copy-start.10
  149.4 8.4 %copy-start.7 = (f32[1024,768]{0,1:T(8,128)}, f32[1024,768]{0,1:T(8,128)S(1)}, u32[]{:S(2)}) copy-start(f32[1024,768]{0,1:T(8,128)S(1)} %fusion.32) | copy-start | bytes 9437188
  151.0 6.8 %copy-start.39 = (bf16[1024,2048]{1,0:T(8,128)(2,1)S(1)}, bf16[1024,2048]{1,0:T(8,128)(2,1)}, u32[]{:S(2)}) copy-start(bf16[1024,2048]{1,0:T(8,128)(2,1)} %get-tuple-element.48) | copy-start | bytes 12582916
  167.0 144.1 %reduce-scatter.9.cloned.1.call-start = ((), (), s32[]{:S(2)}) async-start(), calls=%async_computation.4 | async-start | bytes 4718592 | tf_op jit(solution)/shard_map/reduce_scatter | solution.py:455
  167.1 9.2 %slice-start.2 = ((s8[5242880]{0:T(1024)(128)(4,1)}), s8[1048576]{0:T(1024)(128)(4,1)S(1)}, s32[]{:S(2)}) async-start(s8[5242880]{0:T(1024)(128)(4,1)} %bitcast.39), calls=%async_computation.10 | async-start | bytes 2097152
  167.8 241.1 %reduce-scatter.13.cloned.1.call-start = ((), (), s32[]{:S(2)}) async-start(), calls=%async_computation.6 | async-start | bytes 7798784
  167.9 8.4 %slice-start.3 = ((s8[5242880]{0:T(1024)(128)(4,1)}), s8[4194304]{0:T(1024)(128)(4,1)S(1)}, s32[]{:S(2)}) async-start(s8[5242880]{0:T(1024)(128)(4,1)} %bitcast.39), calls=%async_computation.11 | async-start | bytes 8388608
  167.9 8.4 %copy-start.11 = (bf16[1024,1024]{1,0:T(8,128)(2,1)S(1)}, bf16[1024,1024]{1,0:T(8,128)(2,1)}, u32[]{:S(2)}) copy-start(bf16[1024,1024]{1,0:T(8,128)(2,1)} %get-tuple-element.47) | copy-start | bytes 6291460
  167.9 8.4 %copy-start.40 = (bf16[1024,2048]{1,0:T(8,128)(2,1)S(1)}, bf16[1024,2048]{1,0:T(8,128)(2,1)}, u32[]{:S(2)}) copy-start(bf16[1024,2048]{1,0:T(8,128)(2,1)} %get-tuple-element.48) | copy-start | bytes 12582916
  200.4 1.0 copy-start.16
  200.4 1.2 copy-start.17
  200.4 1.4 copy-start.18
  202.1 45.4 %copy-start = (bf16[128,2048]{1,0:T(8,128)(2,1)S(1)}, bf16[128,2048]{1,0:T(8,128)(2,1)}, u32[]{:S(2)}) copy-start(bf16[128,2048]{1,0:T(8,128)(2,1)} %x_in.1) | copy-start | bytes 1572868
  204.2 44.2 %copy-start.27 = (f32[2048]{0:T(1024)S(1)}, f32[2048]{0:T(1024)}, u32[]{:S(2)}) copy-start(f32[2048]{0:T(1024)} %get-tuple-element.129) | copy-start | bytes 24580
  204.3 44.2 %copy-start.28 = (f32[2048]{0:T(1024)S(1)}, f32[2048]{0:T(1024)}, u32[]{:S(2)}) copy-start(f32[2048]{0:T(1024)} %get-tuple-element.163) | copy-start | bytes 24580
  204.3 44.3 %copy-start.31 = (f32[3,256]{1,0:T(4,128)S(1)}, f32[3,256]{1,0:T(4,128)}, u32[]{:S(2)}) copy-start(f32[3,256]{1,0:T(4,128)} %b_qkv.1) | copy-start | bytes 9220
  204.3 44.3 %copy-start.32 = (f32[3,256]{1,0:T(4,128)S(1)}, f32[3,256]{1,0:T(4,128)}, u32[]{:S(2)}) copy-start(f32[3,256]{1,0:T(4,128)} %param.47) | copy-start | bytes 9220
  204.3 44.2 %copy-start.33 = (f32[3,256]{1,0:T(4,128)S(1)}, f32[3,256]{1,0:T(4,128)}, u32[]{:S(2)}) copy-start(f32[3,256]{1,0:T(4,128)} %param.46) | copy-start | bytes 9220
  204.3 44.9 %copy-start.34 = (f32[1024]{0:T(1024)S(1)}, f32[1024]{0:T(1024)}, u32[]{:S(2)}) copy-start(f32[1024]{0:T(1024)} %param.35) | copy-start | bytes 12292
  204.3 44.9 %copy-start.35 = (f32[1024]{0:T(1024)S(1)}, f32[1024]{0:T(1024)}, u32[]{:S(2)}) copy-start(f32[1024]{0:T(1024)} %param.49) | copy-start | bytes 12292
  204.3 44.8 %copy-start.36 = (f32[1024]{0:T(1024)S(1)}, f32[1024]{0:T(1024)}, u32[]{:S(2)}) copy-start(f32[1024]{0:T(1024)} %param.48) | copy-start | bytes 12292
  204.4 48.6 %copy-start.13 = (f32[1024,128]{1,0:T(8,128)S(1)}, f32[1024,128]{1,0:T(8,128)}, u32[]{:S(2)}) copy-start(f32[1024,128]{1,0:T(8,128)} %w_down.1) | copy-start | bytes 1572868
  204.4 48.6 %copy-start.14 = (f32[1024,128]{1,0:T(8,128)S(1)}, f32[1024,128]{1,0:T(8,128)}, u32[]{:S(2)}) copy-start(f32[1024,128]{1,0:T(8,128)} %param.45) | copy-start | bytes 1572868
  247.7 0.8 copy-start.29
  251.0 6.3 %copy-start.30 = (f32[128]{0:T(128)S(1)}, f32[128]{0:T(128)}, u32[]{:S(2)}) copy-start(f32[128]{0:T(128)} %copy-done.29) | copy-start | bytes 1540
  251.1 6.3 %copy-start.37 = (f32[128]{0:T(128)S(1)}, f32[128]{0:T(128)}, u32[]{:S(2)}) copy-start(f32[128]{0:T(128)} %add_rsqrt_fusion) | copy-start | bytes 1540
  252.9 61.4 %copy-start.25 = (f32[2048]{0:T(1024)S(1)}, f32[2048]{0:T(1024)}, u32[]{:S(2)}) copy-start(f32[2048]{0:T(1024)} %get-tuple-element.128) | copy-start | bytes 24580
  252.9 61.4 %copy-start.26 = (f32[2048]{0:T(1024)S(1)}, f32[2048]{0:T(1024)}, u32[]{:S(2)}) copy-start(f32[2048]{0:T(1024)} %get-tuple-element.164) | copy-start | bytes 24580
  252.9 130.3 %copy-start.23 = (f32[2,2048]{1,0:T(2,128)S(1)}, f32[2,2048]{1,0:T(2,128)}, u32[]{:S(2)}) copy-start(f32[2,2048]{1,0:T(2,128)} %param.51) | copy-start | bytes 49156
  252.9 130.3 %copy-start.24 = (f32[2,2048]{1,0:T(2,128)S(1)}, f32[2,2048]{1,0:T(2,128)}, u32[]{:S(2)}) copy-start(f32[2,2048]{1,0:T(2,128)} %param.50) | copy-start | bytes 49156
  253.0 131.0 %copy-start.21 = (f32[4,2048]{1,0:T(4,128)S(1)}, f32[4,2048]{1,0:T(4,128)}, u32[]{:S(2)}) copy-start(f32[4,2048]{1,0:T(4,128)} %param.53) | copy-start | bytes 98308
  253.0 131.0 %copy-start.22 = (f32[4,2048]{1,0:T(4,128)S(1)}, f32[4,2048]{1,0:T(4,128)}, u32[]{:S(2)}) copy-start(f32[4,2048]{1,0:T(4,128)} %param.52) | copy-start | bytes 98308
  410.2 7.3 %copy-start.12 = (f32[128,3,256]{2,0,1:T(8,128)S(1)}, f32[128,3,256]{2,0,1:T(8,128)}, u32[]{:S(2)}) copy-start(f32[128,3,256]{2,0,1:T(8,128)} %param.30) | copy-start | bytes 1179652
  (1 other events, 0.8 us)
Sparse Core Ops, SparseCore 0:
  117.1 85.1 reduce-scatter.14
  204.8 52.5 reduce-scatter.10
  259.8 51.3 reduce-scatter.8
  315.2 93.5 reduce-scatter.12

commit v2 on v1

--- a/solution.py
+++ b/solution.py
@@ -425,6 +425,491 @@
     return lax.dot_general(left, right, (((1,), (1,)), ((), ())), preferred_element_type=F32)
 
 
+class Scatter:
+    def __init__(self, links, part, slots, last, z, ring, z_dev, plus, minus):
+        self.links, self.part, self.slots, self.last = links, part, slots, last
+        self.ring, self.z_dev, self.plus, self.minus = ring, z_dev, plus, minus
+        self.zs = (1 - z, z)
+        self.sent = {}
+
+    def push(self, way, message, order, ring, half):
+        self.sent[way, message, order] = self.links.send(
+            self.part(self.zs[order], ring, half),
+            self.slots.at[way, message, order],
+            self.minus if way else self.plus,
+        )
+
+    def arrived(self, way, message, order):
+        self.sent[way, message, order].wait_recv()
+        return self.slots[way, message, order].astype(F32)
+
+    def far(self):
+        for order in range(2):
+            self.push(0, 0, order, around(self.ring, 2), 0)
+            self.push(1, 0, order, around(self.ring, 2), 1)
+
+    def near(self, way):
+        for order in range(2):
+            self.push(way, 1, order, around(self.ring, -1 if way else 1), 1 - way)
+
+    def join(self, order):
+        for way in range(2):
+            ring = around(self.ring, -1 if way else 1)
+            part = self.part(self.zs[order], ring, way)
+            part[...] = (part[...].astype(F32) + self.arrived(way, 0, order)).astype(BF16)
+            self.push(way, 2, order, ring, way)
+
+    def total(self, order, half):
+        part = self.part(self.zs[order], self.ring, half)
+        return (
+            part[...].astype(F32) + self.arrived(half, 2, order) + self.arrived(1 - half, 1, order)
+        )
+
+    def partner(self):
+        for half in range(2):
+            part = self.part(self.zs[0], self.ring, half)
+            part[...] = self.total(0, half).astype(BF16)
+        self.by_z = self.links.send(
+            self.part(self.zs[0], self.ring, None), self.last, self.z_dev
+        )
+
+    def finish(self, out):
+        sums = [self.total(1, half) for half in range(2)]
+        self.by_z.wait_recv()
+        rows = out.shape[0] // 2
+        for half in range(2):
+            part = pl.ds(half * rows, rows)
+            out[part, :] = sums[half] + self.last[part, :].astype(F32)
+
+
+def backward_kernel(
+    unit_in,
+    cot_in,
+    wide_in,
+    deep_in,
+    q_in,
+    k_in,
+    v_in,
+    acts_in,
+    slope_in,
+    probs_in,
+    turn_in,
+    branch_in,
+    gains,
+    biases,
+    branch_sum,
+    unit_sum,
+    wide_sum,
+    deep_sum,
+    vector_sum,
+    unit,
+    cot,
+    wide,
+    deep,
+    q,
+    k,
+    v,
+    acts,
+    probs,
+    turn,
+    branch,
+    grads,
+    mixed_grad,
+    pair,
+    normed,
+    sums,
+    low_sums,
+    vectors,
+    vector_slots,
+    wide_core,
+    deep_core,
+    wide_slots,
+    deep_slots,
+    branch_slots,
+    unit_slots,
+    wide_last,
+    deep_last,
+    branch_last,
+    unit_last,
+    row_total,
+    wide_total,
+    deep_total,
+    send_sems,
+    recv_sems,
+    core_send,
+    core_recv,
+    load_sems,
+    store_sems,
+):
+    spot = place()
+    zh, y, core, zl, x = spot
+    near = neighbours(spot)
+    near["x2"] = device(zh, y, core, zl, around(x, 2))
+    near["y2"] = device(zh, around(y, 2), core, zl, x)
+    barrier = pltpu.get_barrier_semaphore()
+    for target in near.values():
+        pl.semaphore_signal(barrier, inc=1, device_id=target, device_id_type=MESH)
+
+    loads = {}
+    for name, src, dst in (
+        ("branch", branch_in, branch),
+        ("cot", cot_in, cot),
+        ("deep", deep_in, deep),
+        ("slope", slope_in, grads.at[:, pl.ds(QKV, UNITS)]),
+        ("acts", acts_in, acts),
+        ("probs", probs_in, probs),
+        ("v", v_in, v),
+        ("k", k_in, k),
+        ("q", q_in, q),
+        ("turn", turn_in, turn),
+        ("unit", unit_in, unit),
+        ("wide", wide_in, wide),
+    ):
+        loads[name] = pltpu.make_async_copy(src, dst, load_sems.at[len(loads)])
+        loads[name].start()
+
+    links = Links(send_sems, recv_sems)
+    stores = []
+
+    def store(src, dst):
+        copy = pltpu.make_async_copy(src, dst, store_sems.at[len(stores)])
+        copy.start()
+        stores.append(copy)
+        return copy
+
+    def token_part(ref):
+        def part(z, ring, half):
+            start = (z * 4 + ring) * OWN
+            if half is None:
+                return rows_of(ref, start, OWN)
+            return rows_of(ref, start + half * (OWN // 2), OWN // 2)
+
+        return part
+
+    def wide_part(z, ring, half):
+        start = ((z * 4 + ring) * 2 + core) * OWN
+        if half is None:
+            return rows_of(wide, start, OWN)
+        return rows_of(wide, start + half * (OWN // 2), OWN // 2)
+
+    def deep_part(z, ring, half):
+        columns = pl.ds(pl.multiple_of(((z * 4 + ring) * 2 + core) * OWN, OWN), OWN)
+        if half is None:
+            return deep.at[:, columns]
+        return deep.at[pl.ds(half * (DEEP // 2), DEEP // 2), columns]
+
+    tensor_ends = (zl, x, near["zl"], near["x+"], near["x-"])
+    data_ends = (zh, y, near["zh"], near["y+"], near["y-"])
+    branches = Scatter(links, token_part(branch), branch_slots, branch_last, *tensor_ends)
+    units = Scatter(links, token_part(cot), unit_slots, unit_last, *tensor_ends)
+    wides = Scatter(links, wide_part, wide_slots, wide_last, *data_ends)
+    deeps = Scatter(links, deep_part, deep_slots, deep_last, *data_ends)
+
+    def core_copy(which, buffer, slots, place_of, ring, turn_of):
+        number = which * 8 + ring * 2 + turn_of
+        z = zh + (1 - 2 * zh) * turn_of
+        chip = z * 4 + around(y, ring)
+        return pltpu.make_async_remote_copy(
+            src_ref=place_of(buffer, chip, 1 - core),
+            dst_ref=slots.at[ring * 2 + turn_of],
+            send_sem=core_send.at[number],
+            recv_sem=core_recv.at[number],
+            device_id=near["core"],
+            device_id_type=MESH,
+        )
+
+    def deep_place(ref, chip, who):
+        return ref.at[:, pl.ds(pl.multiple_of((chip * 2 + who) * OWN, OWN), OWN)]
+
+    def wide_place(ref, chip, who):
+        return rows_of(ref, (chip * 2 + who) * OWN, OWN)
+
+    def core_add(which, buffer, slots, place_of, ring):
+        def one(turn_of, _):
+            core_copy(which, buffer, slots, place_of, ring, turn_of).wait_recv()
+            z = zh + (1 - 2 * zh) * turn_of
+            mine = place_of(buffer, z * 4 + around(y, ring), core)
+            mine[...] = (
+                mine[...].astype(F32) + slots[ring * 2 + turn_of].astype(F32)
+            ).astype(BF16)
+            return 0
+
+        lax.fori_loop(0, 2, one, 0)
+
+    pl.semaphore_wait(barrier, len(near))
+    loads["branch"].wait()
+    branches.far()
+
+    sums[...] = jnp.zeros_like(sums)
+    low_sums[...] = jnp.zeros_like(low_sums)
+    for name in ("cot", "deep", "slope"):
+        loads[name].wait()
+
+    def back(tile, _):
+        part = pl.ds(pl.multiple_of(tile * TILE, TILE), TILE)
+        mixed_grad[part, :] = by_rows(cot[part, :], deep[:HEAD, :]).astype(BF16)
+
+        def hidden(piece, _):
+            shift = pl.multiple_of(piece * 256, 256)
+            columns = pl.ds(QKV + shift, 256)
+            grad = by_rows(cot[part, :], deep[pl.ds(HEAD + shift, 256), :])
+            grad = grad * grads[part, columns].astype(F32)
+            low_sums[0:1, columns] += jnp.sum(grad, axis=0, keepdims=True)
+            grads[part, columns] = grad.astype(BF16)
+            return 0
+
+        return lax.fori_loop(0, UNITS // 256, hidden, 0)
+
+    lax.fori_loop(0, TOK // TILE, back, 0)
+    branches.near(0)
+    branches.near(1)
+    loads["acts"].wait()
+
+    for index, ring in enumerate((2, 1, 3, 0)):
+
+        def deep_tile(turn_of, _):
+            z = zh + (1 - 2 * zh) * turn_of
+            columns = pl.ds(pl.multiple_of((z * 4 + around(y, ring)) * 256, 256), 256)
+            deep[:, columns] = over_rows(acts[...], cot[:, columns]).astype(BF16)
+            core_copy(0, deep, deep_core, deep_place, ring, turn_of).start()
+            return 0
+
+        lax.fori_loop(0, 2, deep_tile, 0)
+        if index == 1:
+            core_add(0, deep, deep_core, deep_place, 2)
+            deeps.far()
+        elif index == 2:
+            core_add(0, deep, deep_core, deep_place, 1)
+            deeps.near(0)
+        elif index == 3:
+            core_add(0, deep, deep_core, deep_place, 3)
+            deeps.near(1)
+    mine = pl.ds(pl.multiple_of((zl * 4 + x) * OWN, OWN), OWN)
+    sums[4:5, :] = jnp.sum(cot[mine, :].astype(F32), axis=0, keepdims=True)
+    core_add(0, deep, deep_core, deep_place, 0)
+    branches.join(0)
+    branches.join(1)
+
+    for name in ("probs", "v", "k", "q", "turn"):
+        loads[name].wait()
+    for block in range(TOK // QROWS):
+        part = slice(block * QROWS, (block + 1) * QROWS)
+        grad = over_rows(probs[block * QROWS :, part], mixed_grad[block * QROWS :, :])
+        low_sums[0:1, 2 * HEAD : QKV] += jnp.sum(grad, axis=0, keepdims=True)
+        grads[part, 2 * HEAD : QKV] = grad.astype(BF16)
+    for block in range(TOK // QROWS):
+        part = slice(block * QROWS, (block + 1) * QROWS)
+        keys = (block + 1) * QROWS
+        share = probs[part, :keys].astype(F32)
+        prob_grad = by_rows(mixed_grad[part, :], v[:keys, :])
+        delta = jnp.sum(share * prob_grad, axis=-1, keepdims=True)
+        score_grad = (share * (prob_grad - delta)).astype(BF16)
+        probs[part, :keys] = score_grad
+        grad = jnp.dot(score_grad, k[:keys, :], preferred_element_type=F32) * (HEAD**-0.5)
+        grad = spin(grad, turn[0, part, :], turn[1, part, :], True)
+        low_sums[0:1, :HEAD] += jnp.sum(grad, axis=0, keepdims=True)
+        grads[part, :HEAD] = grad.astype(BF16)
+    for block in range(TOK // QROWS):
+        part = slice(block * QROWS, (block + 1) * QROWS)
+        grad = over_rows(probs[block * QROWS :, part], q[block * QROWS :, :]) * (HEAD**-0.5)
+        grad = spin(grad, turn[0, part, :], turn[1, part, :], True)
+        low_sums[0:1, HEAD : 2 * HEAD] += jnp.sum(grad, axis=0, keepdims=True)
+        grads[part, HEAD : 2 * HEAD] = grad.astype(BF16)
+    deeps.join(0)
+    deeps.join(1)
+    loads["unit"].wait()
+    loads["wide"].wait()
+
+    for ring in (2, 1, 3, 0):
+        starts = (around(x, ring) * OWN, (4 + around(x, ring)) * OWN)
+        pieces = [pl.ds(pl.multiple_of(start, OWN), OWN) for start in starts]
+        for half in range(2):
+            pair[half * OWN : (half + 1) * OWN, :] = grads[pieces[half], :]
+
+        def unit_tile(step, _):
+            columns = pl.ds(pl.multiple_of(step * 512, 512), 512)
+            first = by_rows(pair[:, :QKV], wide[columns, :QKV])
+            second = by_rows(pair[:, QKV:], wide[columns, QKV:])
+            rows = jnp.concatenate([unit[piece, columns] for piece in pieces], axis=0).astype(F32)
+            sums[0:1, columns] += jnp.sum(first * rows, axis=0, keepdims=True)
+            sums[1:2, columns] += jnp.sum(second * rows, axis=0, keepdims=True)
+            sums[2:3, columns] += jnp.sum(first, axis=0, keepdims=True)
+            sums[3:4, columns] += jnp.sum(second, axis=0, keepdims=True)
+            both = (first * gains[0:1, columns] + second * gains[1:2, columns]).astype(BF16)
+            cot[pieces[0], columns] = both[:OWN]
+            cot[pieces[1], columns] = both[OWN:]
+            return 0
+
+        lax.fori_loop(0, D // 512, unit_tile, 0)
+        if ring == 2:
+            units.far()
+        elif ring != 0:
+            units.near(0 if ring == 1 else 1)
+    deeps.partner()
+
+    for row in range(5):
+        for column in range(16):
+            vectors[0, row * 16 + column : row * 16 + column + 1, :] = sums[
+                row : row + 1, column * 128 : (column + 1) * 128
+            ]
+    for column in range(14):
+        vectors[0, 80 + column : 81 + column, :] = low_sums[0:1, column * 128 : (column + 1) * 128]
+    vectors[0, 94:96, :] = jnp.zeros((2, 128), F32)
+
+    def swap(stage, first_slot, names, count):
+        rows = pl.ds(0, count)
+        return [
+            links.send(
+                vectors.at[stage, rows], vector_slots.at[first_slot + index, rows], near[name]
+            )
+            for index, name in enumerate(names)
+        ]
+
+    def combine(stage, first_slot, copies, count):
+        for copy in copies:
+            copy.wait_recv()
+        parts = [vectors[stage, :count, :]]
+        parts += [vector_slots[first_slot + index, :count, :] for index in range(len(copies))]
+        if len(parts) == 2:
+            result = parts[0] + parts[1]
+        else:
+            result = (parts[0] + parts[3]) + (parts[1] + parts[2])
+        vectors[stage + 1, :count, :] = result
+
+    moving = swap(0, 0, ("core",), 96)
+
+    for index, ring in enumerate((2, 1, 3, 0)):
+
+        def wide_tile(turn_of, _):
+            z = zh + (1 - 2 * zh) * turn_of
+            span = pl.ds(pl.multiple_of((z * 4 + around(y, ring)) * 256, 256), 256)
+            rows = unit[:, span].astype(F32)
+            normed[0] = (rows * gains[0:1, span] + biases[0:1, span]).astype(BF16)
+            normed[1] = (rows * gains[1:2, span] + biases[1:2, span]).astype(BF16)
+            wide[span, :QKV] = over_rows(normed[0], grads[:, :QKV]).astype(BF16)
+            wide[span, QKV:] = over_rows(normed[1], grads[:, QKV:]).astype(BF16)
+            core_copy(1, wide, wide_core, wide_place, ring, turn_of).start()
+            return 0
+
+        lax.fori_loop(0, 2, wide_tile, 0)
+        if index == 0:
+            combine(0, 0, moving, 96)
+            moving = swap(1, 1, ("y+", "y-", "y2"), 96)
+        elif index == 1:
+            core_add(1, wide, wide_core, wide_place, 2)
+            wides.far()
+            combine(1, 1, moving, 96)
+            moving = swap(2, 4, ("zh",), 96)
+        elif index == 2:
+            core_add(1, wide, wide_core, wide_place, 1)
+            wides.near(0)
+            combine(2, 4, moving, 96)
+            store(vectors.at[3, pl.ds(80, 16)], vector_sum.at[pl.ds(80, 16)])
+            moving = swap(3, 5, ("zl",), 80)
+            branches.partner()
+        elif index == 3:
+            core_add(1, wide, wide_core, wide_place, 3)
+            wides.near(1)
+            combine(3, 5, moving, 80)
+            moving = swap(4, 6, ("x+", "x-", "x2"), 80)
+    core_add(1, wide, wide_core, wide_place, 0)
+    deeps.finish(deep_total)
+    store(deep_total, deep_sum)
+    units.join(0)
+    wides.join(0)
+    units.join(1)
+    wides.join(1)
+    combine(4, 6, moving, 80)
+    store(vectors.at[5, pl.ds(0, 80)], vector_sum.at[pl.ds(0, 80)])
+    branches.finish(row_total)
+    branch_store = store(row_total, branch_sum)
+    wides.partner()
+    units.partner()
+    wides.finish(wide_total)
+    store(wide_total, wide_sum)
+    branch_store.wait()
+    units.finish(row_total)
+    store(row_total, unit_sum)
+
+    for which, buffer, slots, place_of in (
+        (0, deep, deep_core, deep_place),
+        (1, wide, wide_core, wide_place),
+    ):
+        for ring in range(4):
+            for turn_of in range(2):
+                core_copy(which, buffer, slots, place_of, ring, turn_of).wait_send()
+    for copy in stores:
+        if copy is not branch_store:
+            copy.wait()
+    links.drain()
+
+
+SUMS = (
+    ((OWN, D), F32),
+    ((OWN, D), F32),
+    ((OWN, WIDE), F32),
+    ((DEEP, OWN), F32),
+    ((96, 128), F32),
+)
+
+
+def run_backward(kept, gains, biases):
+    anywhere = pl.BlockSpec(memory_space=pl.ANY)
+    vmem = pl.BlockSpec(memory_space=pltpu.VMEM)
+    half = OWN // 2
+    return pl.pallas_call(
+        backward_kernel,
+        out_shape=[jax.ShapeDtypeStruct(*each) for each in SUMS],
+        in_specs=[anywhere] * len(kept) + [vmem, vmem],
+        out_specs=[anywhere] * len(SUMS),
+        scratch_shapes=[
+            pltpu.VMEM((TOK, D), BF16),
+            pltpu.VMEM((TOK, D), BF16),
+            pltpu.VMEM((D, WIDE), BF16),
+            pltpu.VMEM((DEEP, D), BF16),
+            pltpu.VMEM((TOK, HEAD), BF16),
+            pltpu.VMEM((TOK, HEAD), BF16),
+            pltpu.VMEM((TOK, HEAD), BF16),
+            pltpu.VMEM((TOK, DEEP), BF16),
+            pltpu.VMEM((TOK, TOK), BF16),
+            pltpu.VMEM((2, TOK, 128), F32),
+            pltpu.VMEM((TOK, D), BF16),
+            pltpu.VMEM((TOK, WIDE), BF16),
+            pltpu.VMEM((TOK, HEAD), BF16),
+            pltpu.VMEM((2 * OWN, WIDE), BF16),
+            pltpu.VMEM((2, TOK, 256), BF16),
+            pltpu.VMEM((8, D), F32),
+            pltpu.VMEM((8, WIDE), F32),
+            pltpu.VMEM((6, 96, 128), F32),
+            pltpu.VMEM((9, 96, 128), F32),
+            pltpu.VMEM((8, OWN, WIDE), BF16),
+            pltpu.VMEM((8, DEEP, OWN), BF16),
+            pltpu.VMEM((2, 3, 2, half, WIDE), BF16),
+            pltpu.VMEM((2, 3, 2, DEEP // 2, OWN), BF16),
+            pltpu.VMEM((2, 3, 2, half, D), BF16),
+            pltpu.VMEM((2, 3, 2, half, D), BF16),
+            pltpu.VMEM((OWN, WIDE), BF16),
+            pltpu.VMEM((DEEP, OWN), BF16),
+            pltpu.VMEM((OWN, D), BF16),
+            pltpu.VMEM((OWN, D), BF16),
+            pltpu.VMEM((OWN, D), F32),
+            pltpu.VMEM((OWN, WIDE), F32),
+            pltpu.VMEM((DEEP, OWN), F32),
+            pltpu.SemaphoreType.DMA((64,)),
+            pltpu.SemaphoreType.DMA((64,)),
+            pltpu.SemaphoreType.DMA((16,)),
+            pltpu.SemaphoreType.DMA((16,)),
+            pltpu.SemaphoreType.DMA((len(kept),)),
+            pltpu.SemaphoreType.DMA((8,)),
+        ],
+        compiler_params=pltpu.CompilerParams(
+            collective_id=1, has_side_effects=True, vmem_limit_bytes=63 * 2**20
+        ),
+        cost_estimate=pl.CostEstimate(flops=28 * 10**9, bytes_accessed=40 * 10**6, transcendentals=0),
+        name="backward",
+    )(*kept, gains, biases)
+
+
 def adam_step(weight, gradient, moment_one, moment_two, step_rate, decay_rate):
     moment_one = BETA_ONE * moment_one + (1.0 - BETA_ONE) * gradient
     moment_two = BETA_TWO * moment_two + (1.0 - BETA_TWO) * gradient * gradient
@@ -436,89 +921,63 @@
     return (moment_one, moment_two, weight - step_rate * (ratio + decay_rate * weight))
 
 
-def local(
-    layer_in, cotangent, seq_lengths, w_qkv, w_out, w_up, w_down, b_qkv, b_up, norm_gains, row_biases,
-    m_qkv, v_qkv, m_out, v_out, m_up, v_up, m_down, v_down, m_bqkv, v_bqkv, m_bup, v_bup,
-    m_gains, v_gains, m_biases, v_biases,
-):
-    tensor_size = lax.axis_size("tensor")
-    tensor_place = lax.axis_index("tensor")
+def local(layer_in, cotangent, seq_lengths, *state):
+    params, moments = state[:8], state[8:]
+    w_qkv, w_out, w_up, w_down, b_qkv, b_up, norm_gains, row_biases = params
     resid = layer_in.astype(F32)
-    row_mean = jnp.mean(resid, axis=-1, keepdims=True)
-    centered = resid - row_mean
+    centered = resid - jnp.mean(resid, axis=-1, keepdims=True)
     variance = jnp.mean(centered * centered, axis=-1, keepdims=True)
     inverse = lax.rsqrt(variance + NORM_EPS)
     own_unit = centered * inverse
-    (unit, grad_rows, wide, deep, q, k, v, acts, slope, probs, turn, branch) = run_forward(
-        seq_lengths, layer_in, cotangent, w_qkv.reshape(OWN, QKV), w_out, w_up, w_down,
-        b_qkv, b_up.reshape(1, UNITS), norm_gains, row_biases)
-    branch = lax.psum_scatter(branch, "tensor", scatter_dimension=0, tiled=True).astype(F32)
+    kept = run_forward(
+        seq_lengths,
+        layer_in,
+        cotangent,
+        w_qkv.reshape(OWN, QKV),
+        w_out,
+        w_up,
+        w_down,
+        b_qkv,
+        b_up.reshape(1, UNITS),
+        norm_gains,
+        row_biases,
+    )
+    branch, unit_grad, wide_sum, deep_sum, vector_sum = run_backward(kept, norm_gains, row_biases)
     out_rows = (resid + branch + row_biases[2] + row_biases[3]).astype(BF16)
-    deep_grad = over_rows(acts, grad_rows)
-    back = by_rows(grad_rows, deep)
-    mixed_grad = back[:, :HEAD].astype(BF16)
-    inner_grad = back[:, HEAD:] * slope.astype(F32)
-    inner_low = inner_grad.astype(BF16)
-    unit_f = unit.astype(F32)
-    first_normed = (unit_f * norm_gains[0] + row_biases[0]).astype(BF16)
-    second_normed = (unit_f * norm_gains[1] + row_biases[1]).astype(BF16)
-    up_grad = over_rows(second_normed, inner_low)
-    second_part = by_rows(inner_low, wide[:, QKV:])
-    index = jnp.arange(TOK)
-    pf = jnp.where(index[:, None] // QROWS >= index[None, :] // QROWS, probs.astype(F32), 0.0)
-    prob_grad = by_rows(mixed_grad, v)
-    delta = jnp.sum(pf * prob_grad, axis=-1, keepdims=True)
-    score_grad = (pf * (prob_grad - delta)).astype(BF16)
-    scale = HEAD**-0.5
-    query_grad = jnp.dot(score_grad, k, preferred_element_type=F32) * scale
-    key_grad = over_rows(score_grad, q) * scale
-    value_grad = over_rows(pf.astype(BF16), mixed_grad)
-
-    def back_spin(rows):
-        cosines, sines = turn[0, :, :64], turn[1, :, :64]
-        sined = rows[:, :64] * sines
-        turned = jnp.concatenate([sined[:, 32:], -sined[:, :32]], axis=1)
-        return jnp.concatenate([rows[:, :64] * cosines + turned, rows[:, 64:]], axis=1)
-
-    projected_grad = jnp.concatenate([back_spin(query_grad), back_spin(key_grad), value_grad], axis=1)
-    projected_low = projected_grad.astype(BF16)
-    qkv_grad = over_rows(first_normed, projected_low)
-    first_part = by_rows(projected_low, wide[:, :QKV])
-    qkv_bias_grad = jnp.sum(projected_grad, axis=0).reshape(3, HEAD)
-    up_bias_grad = jnp.sum(inner_grad, axis=0)
-    grad_own = cotangent.astype(F32)
-    out_bias_grad = jnp.sum(grad_own, axis=0)
-    gain_part = jnp.stack([jnp.sum(first_part * unit_f, axis=0), jnp.sum(second_part * unit_f, axis=0)])
-    shift_part = jnp.stack([jnp.sum(first_part, axis=0), jnp.sum(second_part, axis=0)])
-    unit_grad = lax.psum_scatter(
-        (first_part * norm_gains[0] + second_part * norm_gains[1]).astype(BF16),
-        "tensor", scatter_dimension=0, tiled=True).astype(F32)
     unit_mean = jnp.mean(unit_grad, axis=-1, keepdims=True)
     unit_proj = jnp.mean(unit_grad * own_unit, axis=-1, keepdims=True)
-    input_grad = grad_own + inverse * (unit_grad - unit_mean - own_unit * unit_proj)
-    bias_part = jnp.concatenate([shift_part, out_bias_grad[None, :], out_bias_grad[None, :]], axis=0)
-    gain_sum, bias_sum = lax.psum((gain_part, bias_part), ("dp", "tensor"))
-    qkv_bias_sum, up_bias_sum = lax.psum((qkv_bias_grad, up_bias_grad), "dp")
-    wide_grad = jnp.concatenate([qkv_grad, up_grad], axis=1).astype(BF16)
-    wide_sum = lax.psum_scatter(wide_grad, "dp", scatter_dimension=0, tiled=True).astype(F32)
-    deep_sum = lax.psum_scatter(deep_grad.astype(BF16), "dp", scatter_dimension=1, tiled=True).astype(F32)
-    params = (w_qkv, w_out, w_up, w_down, b_qkv, b_up, norm_gains, row_biases)
-    grad_list = (wide_sum[:, :QKV].reshape(OWN, 3, HEAD), deep_sum[:HEAD], wide_sum[:, QKV:], deep_sum[HEAD:],
-                 qkv_bias_sum, up_bias_sum, gain_sum, bias_sum)
-    moments = ((m_qkv, v_qkv), (m_out, v_out), (m_up, v_up), (m_down, v_down), (m_bqkv, v_bqkv),
-               (m_bup, v_bup), (m_gains, v_gains), (m_biases, v_biases))
+    input_grad = cotangent.astype(F32) + inverse * (unit_grad - unit_mean - own_unit * unit_proj)
+    vectors = vector_sum[:80].reshape(5, D)
+    low_vectors = vector_sum[80:94].reshape(WIDE)
+    grad_list = (
+        wide_sum[:, :QKV].reshape(OWN, 3, HEAD),
+        deep_sum[:HEAD],
+        wide_sum[:, QKV:],
+        deep_sum[HEAD:],
+        low_vectors[:QKV].reshape(3, HEAD),
+        low_vectors[QKV:],
+        vectors[:2],
+        jnp.concatenate([vectors[2:5], vectors[4:5]], axis=0),
+    )
     updated = []
     for which in range(8):
-        updated.extend(adam_step(params[which], grad_list[which], moments[which][0], moments[which][1],
-                                 STEP_RATES[which], DECAY_RATES[which]))
+        updated.extend(
+            adam_step(
+                params[which],
+                grad_list[which],
+                moments[2 * which],
+                moments[2 * which + 1],
+                STEP_RATES[which],
+                DECAY_RATES[which],
+            )
+        )
     return (out_rows, input_grad, *updated)
 
 
 def solution(mesh):
     rows = P(("dp", "tensor"), None)
-    qkv, out, up, down = P("dp", None, "tensor"), P("tensor", "dp"), P("dp", "tensor"), P("tensor", "dp")
-    bqkv, bup = P(None, "tensor"), P("tensor")
-    params = (qkv, out, up, down, bqkv, bup, P(), P())
+    out, up = P("tensor", "dp"), P("dp", "tensor")
+    params = (P("dp", None, "tensor"), out, up, out, P(None, "tensor"), P("tensor"), P(), P())
     moments = [spec for spec in params for _ in range(2)]
     return jax.shard_map(
         local,

time: 432 us -> 215 us (0.50); the launches traced: 427 us -> 215 us
  blocking collectives: 108 us -> 0 us
  Pallas kernels: 89.8 us -> 189 us
  waiting for transfers between devices: 79.2 us -> 0 us
  matrix products: 56.9 us -> 0 us
  local copies, waits for them, and re-layouts: 44.7 us -> 12.6 us
  other arithmetic: 32.9 us -> 12.4 us
  between operations: 14.7 us -> 0.97 us
    psum x2 -> x0, blocking collectives: 108 us -> none  [the longest x1 68.9 us: local(): gain_sum, bias_sum = lax.psum((gain_part, bias_part), ('dp', 'tensor'))]
    pallas_call x0 -> x1, Pallas kernels: none -> 99.3 us  [run_backward(): pl.pallas_call(backward_kernel, out_shape=[jax.ShapeDtypeStruct(*each) fo...]
    dot_general x10 -> x0, matrix products: 56.9 us -> none  [the longest x5 27.9 us: over_rows(): lax.dot_general(left, right, (((0,), (0,)), ((), ())), preferred_element_...]
    reduce_scatter x2 -> x0, waiting for transfers between devices: 54.2 us -> none  [the longest x1 52.4 us: local(): lax.psum_scatter(branch, 'tensor', scatter_dimension=0, tiled=True)]
    unnamed x105 -> x58, local copies, waits for them, and re-layouts: 35.7 us -> 8.94 us
    unnamed x6 -> x0, waiting for transfers between devices: 24.9 us -> none
    reduce_sum x4 -> x1, other arithmetic: 8.96 us -> 0.15 us  [local(): centered = resid - jnp.mean(resid, axis=-1, keepdims=True)]
    concatenate x2 -> x0, other arithmetic: 7.61 us -> none  [the longest x1 7.57 us: local(): wide_grad = jnp.concatenate([qkv_grad, up_grad], axis=1).astype(BF16)]
  transfers between devices with their start and end apart: 4 -> 0, of which waited for: 3 -> 0; matrix products, arithmetic and copies ran while one was open for 23% -> 0% of each run, Pallas kernels for 0% -> 0%
where the time goes in v2:
time: 215 us
  Pallas kernels  189 us (88%)
  local copies, waits for them, and re-layouts  12.6 us (6%)
  other arithmetic  12.4 us (6%)
    pallas_call x1, Pallas kernels, run_backward(): pl.pallas_call(backward_kernel, out_shape=[jax.ShapeDtypeStruct(*each) fo...  99.3 us
    pallas_call x1, Pallas kernels, run_forward(): pl.pallas_call(forward_kernel, out_shape=[jax.ShapeDtypeStruct(*kept) for...  89.4 us
    unnamed x58, local copies, waits for them, and re-layouts  8.94 us
    sub x8, other arithmetic, adam_step(): weight - step_rate * (ratio + decay_rate * weight)  8.35 us

profile of v2, /device:TPU:0, one launch (start us, length us, event | category | flops | bytes accessed | tf_op | source)
XLA Modules:
  0.0 214.7 jit_solution(4974525553853001724)
XLA Ops:
  0.7 1.2 copy.57
  1.8 0.9 copy.58.w_qkv
  2.7 89.4 %forward.1 = (bf16[1024,2048]{1,0:T(8,128)(2,1)}, bf16[1024,2048]{1,0:T(8,128)(2,1)}, bf16[2048,1792]{1,0:T(8,128)(2,1)}, bf16[1280,2048]{1,0:T(8,128)(2,1)}, bf...) custom-call(s32[1,4]{1,0:T(1,128)} %lens.1, ...), custom_call_target="tpu_custom_call" | custom-call | flops 14000000000 | bytes 40000000 | tf_op jit(solution)/shard_map/forward/pallas_call | solution.py:399
  92.2 0.0 copy-start.13
  92.2 0.0 copy-start.15
  92.2 0.0 copy-start.16
  92.2 99.3 %backward.1 = (f32[128,2048]{1,0:T(8,128)}, f32[128,2048]{1,0:T(8,128)}, f32[128,1792]{1,0:T(8,128)}, f32[1280,128]{1,0:T(8,128)}, f32[96,128]{1,0:T(8,128)}) custom-call(bf16[1024,2048]{1,0:T(8,128)(2,1)} %get-tuple-element.43.unit_in, bf16[1024,2048]{1,0:T(8,128)(2,1)} %get-tuple-element.44.cot_in, bf16[2048,1792]{1,0:T(8,128)(2,1)} %get-tuple-element.45.wide_in, ...), custom_call_target="tpu_custom_call" | custom-call | flops 28000000000 | bytes 40000000 | tf_op jit(solution)/shard_map/backward/pallas_call | solution.py:860
  191.6 0.7 slice.64
  192.3 0.7 slice.66
  193.0 0.0 copy-done.15
  193.0 0.7 multiply_subtract_fusion.4
  193.7 1.1 slice.55
  194.8 0.2 copy.60
  195.0 2.0 copy.59
  197.0 1.9 copy.61
  198.9 2.1 multiply_subtract_fusion.2
  201.1 1.9 copy.64
  203.0 0.9 copy.65
  203.9 0.9 copy.66
  204.8 0.2 convert_reduce_fusion
  205.0 0.3 fusion.8
  205.3 0.0 copy-done.1
  205.3 0.3 fusion.21
  205.6 0.0 copy-start.7
  205.6 0.0 copy-start.8
  205.7 0.0 copy-start.9
  205.7 3.3 %fusion.7 = (f32[128,2048]{1,0:T(8,128)}, bf16[128,2048]{1,0:T(8,128)(2,1)}) fusion(bf16[128,2048]{1,0:T(8,128)(2,1)S(1)} %copy-done, f32[128,2048]{1,0:T(8,128)S(1)} %copy-done.1, bf16[128,2048]{1,0:T(8,128)(2,1)} %cot_in.1, f32[128]{0:T(128)S(1)} %get-tuple-element.116, f32[128]{0:T(128)S(1)} %get-tuple-element.117, f32[128]{0:T(128)S(1)} %add_rsqrt_fusion, ...), kind=kLoop, calls=%fused_computation.10 | loop fusion | flops 3407872 | bytes 4737024 | tf_op jit(solution)/shard_map/add | solution.py:949
  209.0 0.0 copy-start.17
  209.0 0.0 copy-start.18
  209.0 0.0 copy-start.19
  209.0 0.0 copy-done.3
  209.0 0.0 copy-done.4
  209.0 0.0 copy-done.5
  209.0 0.0 copy-done.6
  209.0 0.0 copy-start.20
  209.1 0.0 copy-start.21
  209.1 0.0 copy-start.22
  209.1 0.0 copy-start.23
  209.1 0.0 copy-start.24
  209.1 0.0 copy-start.25
  209.1 1.4 multiply_subtract_fusion
  210.5 0.0 copy-done.9
  210.5 1.4 multiply_subtract_fusion.1
  211.9 0.0 copy-done.11
  211.9 0.8 multiply_subtract_fusion.3
  212.8 0.7 multiply_subtract_fusion.5
  213.5 0.6 multiply_subtract_fusion.7
  214.1 0.6 multiply_subtract_fusion.6
  (38 shorter events, 0.1 us)
Async XLA Ops:
  92.2 100.8 %copy-start.13 = (f32[4,2048]{1,0:T(4,128)S(1)}, f32[4,2048]{1,0:T(4,128)}, u32[]{:S(2)}) copy-start(f32[4,2048]{1,0:T(4,128)} %biases.3) | copy-start | bytes 98308
  92.2 100.8 %copy-start.15 = (f32[4,2048]{1,0:T(4,128)S(1)}, f32[4,2048]{1,0:T(4,128)}, u32[]{:S(2)}) copy-start(f32[4,2048]{1,0:T(4,128)} %param.53) | copy-start | bytes 98308
  92.2 100.8 %copy-start.16 = (f32[4,2048]{1,0:T(4,128)S(1)}, f32[4,2048]{1,0:T(4,128)}, u32[]{:S(2)}) copy-start(f32[4,2048]{1,0:T(4,128)} %param.52) | copy-start | bytes 98308
  193.7 11.1 %copy-start = (bf16[128,2048]{1,0:T(8,128)(2,1)S(1)}, bf16[128,2048]{1,0:T(8,128)(2,1)}, u32[]{:S(2)}) copy-start(bf16[128,2048]{1,0:T(8,128)(2,1)} %x_in.1) | copy-start | bytes 1572868
  194.8 10.4 %copy-start.1 = (f32[128,2048]{1,0:T(8,128)S(1)}, f32[128,2048]{1,0:T(8,128)}, u32[]{:S(2)}) copy-start(f32[128,2048]{1,0:T(8,128)} %get-tuple-element.56) | copy-start | bytes 3145732
  203.9 5.1 %copy-start.3 = (f32[1280,128]{1,0:T(8,128)S(1)}, f32[1280,128]{1,0:T(8,128)}, u32[]{:S(2)}) copy-start(f32[1280,128]{1,0:T(8,128)} %get-tuple-element.58) | copy-start | bytes 1966084
  203.9 5.1 %copy-start.4 = (f32[1024,128]{1,0:T(8,128)S(1)}, f32[1024,128]{1,0:T(8,128)}, u32[]{:S(2)}) copy-start(f32[1024,128]{1,0:T(8,128)} %w_down.1) | copy-start | bytes 1572868
  204.8 4.2 %copy-start.5 = (f32[1024,128]{1,0:T(8,128)S(1)}, f32[1024,128]{1,0:T(8,128)}, u32[]{:S(2)}) copy-start(f32[1024,128]{1,0:T(8,128)} %param.45) | copy-start | bytes 1572868
  204.8 4.2 %copy-start.6 = (f32[1024,128]{1,0:T(8,128)S(1)}, f32[1024,128]{1,0:T(8,128)}, u32[]{:S(2)}) copy-start(f32[1024,128]{1,0:T(8,128)} %param.44) | copy-start | bytes 1572868
  205.6 4.9 %copy-start.2 = (f32[128,1792]{1,0:T(8,128)S(1)}, f32[128,1792]{1,0:T(8,128)}, u32[]{:S(2)}) copy-start(f32[128,1792]{1,0:T(8,128)} %get-tuple-element.57) | copy-start | bytes 2752516
  205.6 4.9 %copy-start.7 = (f32[128,1024]{1,0:T(8,128)S(1)}, f32[128,1024]{1,0:T(8,128)}, u32[]{:S(2)}) copy-start(f32[128,1024]{1,0:T(8,128)} %w_up.1) | copy-start | bytes 1572868
  205.6 4.9 %copy-start.8 = (f32[128,1024]{1,0:T(8,128)S(1)}, f32[128,1024]{1,0:T(8,128)}, u32[]{:S(2)}) copy-start(f32[128,1024]{1,0:T(8,128)} %param.43) | copy-start | bytes 1572868
  205.7 4.9 %copy-start.9 = (f32[128,1024]{1,0:T(8,128)S(1)}, f32[128,1024]{1,0:T(8,128)}, u32[]{:S(2)}) copy-start(f32[128,1024]{1,0:T(8,128)} %param.42) | copy-start | bytes 1572868
  208.9 3.0 %copy-start.10 = (f32[256,128]{1,0:T(8,128)S(1)}, f32[256,128]{1,0:T(8,128)}, u32[]{:S(2)}) copy-start(f32[256,128]{1,0:T(8,128)} %w_out.1) | copy-start | bytes 393220
  208.9 3.0 %copy-start.11 = (f32[256,128]{1,0:T(8,128)S(1)}, f32[256,128]{1,0:T(8,128)}, u32[]{:S(2)}) copy-start(f32[256,128]{1,0:T(8,128)} %param.41) | copy-start | bytes 393220
  208.9 3.0 %copy-start.12 = (f32[256,128]{1,0:T(8,128)S(1)}, f32[256,128]{1,0:T(8,128)}, u32[]{:S(2)}) copy-start(f32[256,128]{1,0:T(8,128)} %param.40) | copy-start | bytes 393220
  209.0 3.8 %copy-start.14 = (f32[96,128]{1,0:T(8,128)S(1)}, f32[96,128]{1,0:T(8,128)}, u32[]{:S(2)}) copy-start(f32[96,128]{1,0:T(8,128)} %get-tuple-element.59) | copy-start | bytes 147460
  209.0 3.8 %copy-start.17 = (f32[2,2048]{1,0:T(2,128)S(1)}, f32[2,2048]{1,0:T(2,128)}, u32[]{:S(2)}) copy-start(f32[2,2048]{1,0:T(2,128)} %gains.3) | copy-start | bytes 49156
  209.0 3.8 %copy-start.18 = (f32[2,2048]{1,0:T(2,128)S(1)}, f32[2,2048]{1,0:T(2,128)}, u32[]{:S(2)}) copy-start(f32[2,2048]{1,0:T(2,128)} %param.51) | copy-start | bytes 49156
  209.0 3.8 %copy-start.19 = (f32[2,2048]{1,0:T(2,128)S(1)}, f32[2,2048]{1,0:T(2,128)}, u32[]{:S(2)}) copy-start(f32[2,2048]{1,0:T(2,128)} %param.50) | copy-start | bytes 49156
  209.0 4.4 %copy-start.20 = (f32[3,256]{1,0:T(4,128)S(1)}, f32[3,256]{1,0:T(4,128)}, u32[]{:S(2)}) copy-start(f32[3,256]{1,0:T(4,128)} %b_qkv.1) | copy-start | bytes 9220
  209.1 4.4 %copy-start.21 = (f32[3,256]{1,0:T(4,128)S(1)}, f32[3,256]{1,0:T(4,128)}, u32[]{:S(2)}) copy-start(f32[3,256]{1,0:T(4,128)} %param.47) | copy-start | bytes 9220
  209.1 4.4 %copy-start.22 = (f32[3,256]{1,0:T(4,128)S(1)}, f32[3,256]{1,0:T(4,128)}, u32[]{:S(2)}) copy-start(f32[3,256]{1,0:T(4,128)} %param.46) | copy-start | bytes 9220
  209.1 5.0 %copy-start.23 = (f32[1024]{0:T(1024)S(1)}, f32[1024]{0:T(1024)}, u32[]{:S(2)}) copy-start(f32[1024]{0:T(1024)} %param.35) | copy-start | bytes 12292
  209.1 5.0 %copy-start.24 = (f32[1024]{0:T(1024)S(1)}, f32[1024]{0:T(1024)}, u32[]{:S(2)}) copy-start(f32[1024]{0:T(1024)} %param.49) | copy-start | bytes 12292
  209.1 5.0 %copy-start.25 = (f32[1024]{0:T(1024)S(1)}, f32[1024]{0:T(1024)}, u32[]{:S(2)}) copy-start(f32[1024]{0:T(1024)} %param.48) | copy-start | bytes 12292
